TPU v7x, 128 devices: a whole 4x4x4 slice. The times are simulated.
128 devices in a mesh: dp: 8 (over x, core), list: 16 (over y, z).
Axes of the slice: x: 4, y: 4, z: 4, core: 2. Of those that a mesh axis runs over, the one named last changes fastest.
Arguments:
- vectors: bfloat16 [32768, 768], P(('dp', 'list')), may hold values from -6 to 6
- centroids: bfloat16 [65536, 768], P('list'), may hold values from -6 to 6
- projection: bfloat16 [768, 128], replicated, may hold values from -0.21875 to 0.21875
- list_ids: int32 [32768, 2], replicated, may hold values from 0 to 65535, as said below
Outputs:
- placed: bfloat16 [131072, 128], P(('dp', 'list'))
- lowest_score: float32 [32768], P(('dp', 'list'))
Inputs may be any that keep to these rules, and one draw needn't show every extreme that they name: `list_ids`: each row holds two different list ids. List j belongs to owner device (j % 8) * 16 + j // 4096. Device f holds rows f * 256 to f * 256 + 255; of the 512 ids of these rows at most 8 belong to any one owner device, and in every draw some owner device receives exactly 8 from every device's rows.
All inputs are finite; a program needn't handle non-finite values.
Results may differ from a plain program's by a relative error of at most 0.0039.
Values may be sent and summed in bfloat16 or wider, within the bound.
No kernel may reach another device: no remote copies, remote signals or barrier semaphores. Data moves between devices by JAX's collectives and lax.ppermute only.
A program may use at most 128 MiB of HBM per device.

v0:
```python
import jax
import jax.numpy as jnp
from jax import lax
from jax.sharding import PartitionSpec as P

PREFIX = 256


soar_weight = 1.5
masked_score = 1e30


def local(vectors, centroids, projection, list_ids):
    dp_count = lax.axis_size("dp")
    list_count = lax.axis_size("list")
    device_count = dp_count * list_count
    row_count = vectors.shape[0]
    slot_cap = max(2, 4 * row_count // device_count)
    per_device = centroids.shape[0]
    per_owner = per_device // dp_count
    dp_place = lax.axis_index("dp")
    list_place = lax.axis_index("list")
    flat_place = dp_place * list_count + list_place
    group_ids = lax.dynamic_slice_in_dim(
        list_ids, dp_place * list_count * row_count, list_count * row_count, 0
    )
    group_primary = group_ids[:, 0]
    centroid_prefix = centroids[:, :PREFIX]
    primary = group_primary
    local_index = primary - list_place * per_device
    inside = (local_index >= 0) & (local_index < per_device)
    picked = jnp.take(centroid_prefix, jnp.clip(local_index, 0, per_device - 1), axis=0)
    primary_prefix = lax.psum_scatter(
        jnp.where(inside[:, None], picked.astype(jnp.float32), 0.0).astype(jnp.bfloat16),
        "list",
        scatter_dimension=0,
        tiled=True,
    ).astype(jnp.float32)
    head_prefix = vectors[:, :PREFIX]
    residual = (head_prefix.astype(jnp.float32) - primary_prefix).astype(jnp.bfloat16)
    centroid_square = jnp.sum(jnp.square(centroid_prefix.astype(jnp.float32)), axis=1)
    block_size = min(1024, per_device)
    block_total = per_device // block_size
    head_piece, resid_piece = lax.all_gather((head_prefix, residual), "list", axis=0, tiled=True)
    piece_rows = head_piece.shape[0]
    primary = group_primary
    head_float = head_piece.astype(jnp.float32)
    resid_float = resid_piece.astype(jnp.float32)
    head_square = jnp.sum(head_float * head_float, axis=1)
    cross_term = jnp.sum(resid_float * head_float, axis=1)
    resid_power = jnp.mean(resid_float * resid_float, axis=1) + 1e-06
    stacked = jnp.concatenate([head_piece, resid_piece], axis=0)

    def sweep_block(block_index, lowest):
        block_start = block_index * block_size
        block = lax.dynamic_slice_in_dim(centroid_prefix, block_start, block_size, 0)
        block_square = lax.dynamic_slice_in_dim(centroid_square, block_start, block_size, 0)
        products = lax.dot_general(
            stacked, block, (((1,), (1,)), ((), ())), preferred_element_type=jnp.float32
        )
        dot_head = products[:piece_rows]
        dot_resid = products[piece_rows:]
        distance = head_square[:, None] - 2.0 * dot_head + block_square[None, :]
        along = cross_term[:, None] - dot_resid
        scores = (distance + soar_weight * along * along / (PREFIX * resid_power[:, None])) / PREFIX
        list_global = (
            list_place * per_device + block_start + jnp.arange(block_size, dtype=jnp.int32)
        )
        scores = jnp.where(list_global[None, :] == primary[:, None], masked_score, scores)
        return jnp.minimum(lowest, jnp.min(scores, axis=1))

    partial_value = lax.fori_loop(
        0, block_total, sweep_block, jnp.full((piece_rows,), masked_score, jnp.float32)
    )
    group_lowest = lax.pmin(partial_value, "list")
    lowest_score = lax.dynamic_slice_in_dim(group_lowest, list_place * row_count, row_count, 0)
    own_ids = lax.dynamic_slice_in_dim(list_ids, flat_place * row_count, row_count, 0).reshape(-1)
    own_owner = own_ids % dp_count * list_count + own_ids // per_device
    one_hot = (own_owner[:, None] == jnp.arange(device_count, dtype=jnp.int32)[None, :]).astype(
        jnp.int32
    )
    slot_rank = jnp.sum(one_hot * (jnp.cumsum(one_hot, axis=0) - 1), axis=1)
    slot_index = (own_owner * slot_cap + slot_rank).reshape(row_count, 2)
    payload = jnp.dot(vectors, projection, preferred_element_type=jnp.float32).astype(jnp.bfloat16)
    slot_iota = jnp.arange(device_count * slot_cap, dtype=jnp.int32)
    send_hot = jnp.any(slot_iota[:, None, None] == slot_index[None, :, :], axis=2).astype(
        jnp.bfloat16
    )
    outgoing = jnp.dot(send_hot, payload, preferred_element_type=jnp.float32).astype(jnp.bfloat16)
    received = lax.all_to_all(outgoing, ("dp", "list"), split_axis=0, concat_axis=0, tiled=True)
    all_ids = list_ids.reshape(device_count, -1)
    all_owner = all_ids % dp_count * list_count + all_ids // per_device
    arrivals = (all_owner == flat_place).astype(jnp.int32)
    arrival_rank = jnp.where(arrivals > 0, jnp.cumsum(arrivals, axis=1) - 1, slot_cap)
    rank_match = arrival_rank[:, :, None] == jnp.arange(slot_cap, dtype=jnp.int32)[None, None, :]
    slot_table = (jnp.sum(jnp.where(rank_match, all_ids[:, :, None] + 1, 0), axis=1) - 1).reshape(
        -1
    )
    filled = slot_table >= 0
    owned = lax.dynamic_index_in_dim(
        centroids.reshape(per_owner, dp_count, centroids.shape[1]), dp_place, 1, keepdims=False
    )
    owned_proj = jnp.dot(owned, projection, preferred_element_type=jnp.float32)
    local_index = jnp.clip((slot_table - list_place * per_device) // dp_count, 0, per_owner - 1)
    centroid_rows = jnp.take(owned_proj, local_index, axis=0)
    placed = jnp.where(filled[:, None], received.astype(jnp.float32) - centroid_rows, 0.0).astype(
        jnp.bfloat16
    )
    return (placed, lowest_score)


def solution(mesh):
    return jax.shard_map(
        local,
        mesh=mesh,
        in_specs=(P(("dp", "list"), None), P("list", None), P(), P()),
        out_specs=(P(("dp", "list"), None), P(("dp", "list"))),
        check_vma=False,
    )
```

profile of v0, /device:TPU:0, one launch (start us, length us, event | category | flops | bytes accessed | tf_op | source)
XLA Modules:
  0.0 405.4 jit_solution(4573580991199540267)
XLA Ops:
  7.2 0.9 and_reduce_fusion.1
  8.1 0.1 and_reduce_fusion
  8.2 1.7 slice.45
  9.9 16.9 %gather_fusion.1 = bf16[4096,256]{1,0:T(8,128)(2,1)} fusion(bf16[4096,256]{1,0:T(8,128)(2,1)S(1)} %slice.45, s32[4096]{0:T(1024)S(1)} %broadcast_clamp_fusion), kind=kCustom, calls=%fused_computation.1 | custom fusion | bytes 4210688 | tf_op jit(solution)/shard_map/jit(_take)/gather | solution.py:32
  26.9 5.9 %select_convert_fusion = bf16[4096,256]{1,0:T(8,128)(2,1)} fusion(bf16[4096,256]{1,0:T(8,128)(2,1)} %gather_fusion.1, pred[4096]{0:T(1024)(128)(4,1)S(1)} %get-tuple-element.294, pred[4096]{0:T(1024)(128)(4,1)S(1)} %get-tuple-element.292), kind=kLoop, calls=%fused_computation.26 | loop fusion | flops 4194304 | bytes 4202496 | tf_op jit(solution)/shard_map/convert_element_type | solution.py:34
  32.9 0.6 slice.44
  33.6 8.3 %copy.29 = s32[32768,2]{1,0:T(8,128)} copy(s32[32768,2]{0,1:T(2,128)S(1)} %copy-done.4) | data formatting | bytes 524288 | tf_op args[3]
  42.0 0.9 constant_dynamic-slice_fusion.2
  42.9 0.1 reshape.339
  43.0 0.1 reshape.338
  43.2 0.1 copy.38
  43.3 0.2 fusion.28
  43.6 66.4 %reduce-scatter.2.cloned.1.call-done = bf16[256,256]{1,0:T(8,128)(2,1)} async-done(((bf16[4096,256]{1,0:T(8,128)(2,1)}), bf16[256,256]{1,0:T(8,128)(2,1)}) %reduce-scatter.2.cloned.1.call-update) | async-done | bytes 131088 | tf_op jit(solution)/shard_map/reduce_scatter | solution.py:33
  110.0 1.6 subtract_convert_fusion
  111.7 0.2 fusion.27
  111.9 0.1 reduce_sum.58
  112.0 1.0 fusion.43
  113.2 0.4 fusion.12
  113.6 1.3 fusion.13
  114.9 8.0 %all-to-all-start = ((bf16[128,8,128]{2,1,0:T(8,128)(2,1)}), bf16[128,8,128]{2,1,0:T(8,128)(2,1)S(1)}, u32[]{:S(2)}, u32[]{:S(2)}) async-start(bf16[128,8,128]{2,1,0:T(8,128)(2,1)} %fusion.13), calls=%async_computation | async-start | bytes 524288 | tf_op jit(solution)/shard_map/all_to_all | solution.py:90
  122.9 12.6 %reshape.336 = s32[128,4,128]{2,1,0:T(4,128)S(1)} reshape(s32[32768,2]{1,0:T(8,128)} %copy.29) | data formatting | bytes 524288 | tf_op jit(solution)/shard_map/reshape | solution.py:91
  135.5 12.7 %reshape.335 = s32[128,512]{1,0:T(8,128)S(1)} reshape(s32[32768,2]{1,0:T(8,128)} %copy.29) | data formatting | bytes 524288 | tf_op jit(solution)/shard_map/reshape | solution.py:91
  148.2 0.2 copy.31
  148.4 0.5 fusion.30
  149.0 0.1 copy.36
  149.2 0.3 fusion.36
  149.4 2.2 select_reduce_fusion
  151.7 0.1 sub.143
  151.9 0.1 ge.43
  152.0 4.4 %constant_dynamic-slice_fusion.1 = bf16[512,1,768]{2,1,0:T(2,128)(2,1)S(1)} fusion(bf16[512,8,768]{2,1,0:T(8,128)(2,1)} %bitcast.36, s32[]{:T(128)S(6)} %select_n.173), kind=kLoop, calls=%fused_computation.158 | loop fusion | bytes 1572868 | tf_op jit(solution)/shard_map/jit(dynamic_index_in_dim)/dynamic_slice | solution.py:100
  156.5 0.4 fusion.14
  156.9 2.8 gather_fusion
  159.7 2.2 multiply_reduce_fusion
  161.9 1.0 fusion.18
  163.0 43.5 %all-gather.5.cloned.1.call-done = bf16[4096,256]{1,0:T(8,128)(2,1)} async-done(((bf16[256,256]{1,0:T(8,128)(2,1)}), bf16[4096,256]{1,0:T(8,128)(2,1)}) %all-gather.5.cloned.1.call-update) | async-done | bytes 2097168 | tf_op jit(solution)/shard_map/all_gather | solution.py:44
  206.4 4.1 %fusion.11 = (f32[4096]{0:T(1024)S(1)}, f32[4096]{0:T(1024)S(1)}, f32[4096]{0:T(1024)S(1)}) fusion(bf16[4096,256]{1,0:T(8,128)(2,1)} %all-gather.5.cloned.1.call-done, bf16[4096,256]{1,0:T(8,128)(2,1)} %all-gather.3.cloned.1.call-done), kind=kLoop, calls=%fused_computation.23 | loop fusion | flops 8376320 | bytes 4243456 | tf_op jit(solution)/shard_map/reduce_sum | solution.py:51
  210.6 2.3 pad_maximum_fusion
  212.9 113.2 %while.16 = (s32[]{:T(128)}, f32[4096]{0:T(1024)S(1)}, s32[]{:T(128)}, s32[4096,1]{0,1:T(1,128)S(1)}, f32[4096]{0:T(1024)S(1)}, /*index=5*/bf16[4096,256]{1,0:T(...) while((s32[]{:T(128)}, f32[4096]{0:T(1024)S(1)}, ...), condition=%wide.region_14.15_spmd.clone, body=%wide.region_12.14_spmd.clone.sunk | while | flops 4345308160 | bytes 72011984 | solution.py:72
  212.9 15.3 %convolution_bitcast_fusion.2 = f32[8192,1024]{0,1:T(8,128)} fusion(bf16[8192,256]{1,0:T(8,128)(2,1)} %get-tuple-element.393, bf16[4096,256]{1,0:T(8,128)(2,1)S(1)} %get-tuple-element.392, s32[]{:T(128)S(6)} %select_n.273), kind=kOutput, calls=%fused_computation.3.clone.1 | convolution fusion | flops 4294967296 | bytes 38273028 | tf_op jit(solution)/shard_map/while/body/eval_jaxpr/dot_general | solution.py:58
  228.2 12.9 %fusion.90 = f32[4096]{0:T(1024)S(1)} fusion(f32[8192,1024]{0,1:T(8,128)} %convolution_bitcast_fusion.2, f32[4096]{0:T(1024)S(1)} %broadcast_multiply_fusion.2, f32[4096]{0:T(1024)S(1)} %get-tuple-element.395, f32[1024]{0:T(1024)S(1)} %dynamic_slice.46, f32[4096]{0:T(1024)S(1)} %get-tuple-element.391, s32[4096]{0:T(1024)S(1)} %bitcast.38, ...), kind=kLoop, calls=%fused_computation.12.clone.1 | loop fusion | flops 50327552 | bytes 33644544 | tf_op jit(solution)/shard_map/while/body/eval_jaxpr/reduce_min | solution.py:70
  241.1 15.3 %convolution_bitcast_fusion.2 = f32[8192,1024]{0,1:T(8,128)} fusion(bf16[8192,256]{1,0:T(8,128)(2,1)} %get-tuple-element.393, bf16[4096,256]{1,0:T(8,128)(2,1)S(1)} %get-tuple-element.392, s32[]{:T(128)S(6)} %select_n.273), kind=kOutput, calls=%fused_computation.3.clone.1 | convolution fusion | flops 4294967296 | bytes 38273028 | tf_op jit(solution)/shard_map/while/body/eval_jaxpr/dot_general | solution.py:58
  256.5 12.9 %fusion.90 = f32[4096]{0:T(1024)S(1)} fusion(f32[8192,1024]{0,1:T(8,128)} %convolution_bitcast_fusion.2, f32[4096]{0:T(1024)S(1)} %broadcast_multiply_fusion.2, f32[4096]{0:T(1024)S(1)} %get-tuple-element.395, f32[1024]{0:T(1024)S(1)} %dynamic_slice.46, f32[4096]{0:T(1024)S(1)} %get-tuple-element.391, s32[4096]{0:T(1024)S(1)} %bitcast.38, ...), kind=kLoop, calls=%fused_computation.12.clone.1 | loop fusion | flops 50327552 | bytes 33644544 | tf_op jit(solution)/shard_map/while/body/eval_jaxpr/reduce_min | solution.py:70
  269.5 15.3 %convolution_bitcast_fusion.2 = f32[8192,1024]{0,1:T(8,128)} fusion(bf16[8192,256]{1,0:T(8,128)(2,1)} %get-tuple-element.393, bf16[4096,256]{1,0:T(8,128)(2,1)S(1)} %get-tuple-element.392, s32[]{:T(128)S(6)} %select_n.273), kind=kOutput, calls=%fused_computation.3.clone.1 | convolution fusion | flops 4294967296 | bytes 38273028 | tf_op jit(solution)/shard_map/while/body/eval_jaxpr/dot_general | solution.py:58
  284.8 12.9 %fusion.90 = f32[4096]{0:T(1024)S(1)} fusion(f32[8192,1024]{0,1:T(8,128)} %convolution_bitcast_fusion.2, f32[4096]{0:T(1024)S(1)} %broadcast_multiply_fusion.2, f32[4096]{0:T(1024)S(1)} %get-tuple-element.395, f32[1024]{0:T(1024)S(1)} %dynamic_slice.46, f32[4096]{0:T(1024)S(1)} %get-tuple-element.391, s32[4096]{0:T(1024)S(1)} %bitcast.38, ...), kind=kLoop, calls=%fused_computation.12.clone.1 | loop fusion | flops 50327552 | bytes 33644544 | tf_op jit(solution)/shard_map/while/body/eval_jaxpr/reduce_min | solution.py:70
  297.8 15.3 %convolution_bitcast_fusion.2 = f32[8192,1024]{0,1:T(8,128)} fusion(bf16[8192,256]{1,0:T(8,128)(2,1)} %get-tuple-element.393, bf16[4096,256]{1,0:T(8,128)(2,1)S(1)} %get-tuple-element.392, s32[]{:T(128)S(6)} %select_n.273), kind=kOutput, calls=%fused_computation.3.clone.1 | convolution fusion | flops 4294967296 | bytes 38273028 | tf_op jit(solution)/shard_map/while/body/eval_jaxpr/dot_general | solution.py:58
  313.1 12.9 %fusion.90 = f32[4096]{0:T(1024)S(1)} fusion(f32[8192,1024]{0,1:T(8,128)} %convolution_bitcast_fusion.2, f32[4096]{0:T(1024)S(1)} %broadcast_multiply_fusion.2, f32[4096]{0:T(1024)S(1)} %get-tuple-element.395, f32[1024]{0:T(1024)S(1)} %dynamic_slice.46, f32[4096]{0:T(1024)S(1)} %get-tuple-element.391, s32[4096]{0:T(1024)S(1)} %bitcast.38, ...), kind=kLoop, calls=%fused_computation.12.clone.1 | loop fusion | flops 50327552 | bytes 33644544 | tf_op jit(solution)/shard_map/while/body/eval_jaxpr/reduce_min | solution.py:70
  326.1 72.2 %pmin.7 = f32[4096]{0:T(1024)S(1)} all-reduce(f32[4096]{0:T(1024)S(1)} %get-tuple-element.235), channel_id=1, replica_groups=mesh['dp'=8,'list'=16] {'list'}, use_global_device_ids=true, to_apply=%region_15.16 | all-reduce | flops 4096 | bytes 32768 | tf_op jit(solution)/shard_map/pmin | solution.py:75
  398.3 0.6 dynamic_slice.34
  (58 shorter events, 0.8 us)
Async XLA Ops:
  7.2 106.4 %copy-start = (bf16[768,128]{1,0:T(8,128)(2,1)S(1)}, bf16[768,128]{1,0:T(8,128)(2,1)}, u32[]{:S(2)}) copy-start(bf16[768,128]{1,0:T(8,128)(2,1)} %param.8) | copy-start | bytes 589828
  7.2 102.8 %reduce-scatter.2.cloned.1.call-start = ((), (), s32[]{:S(2)}) async-start(), calls=%async_computation.3 | async-start | bytes 2228224 | tf_op jit(solution)/shard_map/reduce_scatter | solution.py:33
  26.9 6.0 %copy-start.5 = (bf16[256,768]{1,0:T(8,128)(2,1)S(1)}, bf16[256,768]{1,0:T(8,128)(2,1)}, u32[]{:S(2)}) copy-start(bf16[256,768]{1,0:T(8,128)(2,1)} %param.6) | copy-start | bytes 1179652
  26.9 6.8 %copy-start.4 = (s32[32768,2]{0,1:T(2,128)S(1)}, s32[32768,2]{0,1:T(2,128)}, u32[]{:S(2)}) copy-start(s32[32768,2]{0,1:T(2,128)} %param.9) | copy-start | bytes 786436
  32.8 130.1 %all-gather.3.cloned.1.call-start = ((), (), s32[]{:S(2)}) async-start(), calls=%async_computation.2 | async-start | bytes 2228224 | tf_op jit(solution)/shard_map/all_gather | solution.py:44
  33.6 172.9 %all-gather.5.cloned.1.call-start = ((), (), s32[]{:S(2)}) async-start(), calls=%async_computation.4 | async-start | bytes 2228224 | tf_op jit(solution)/shard_map/all_gather | solution.py:44
  114.9 47.0 %all-to-all-start = ((bf16[128,8,128]{2,1,0:T(8,128)(2,1)}), bf16[128,8,128]{2,1,0:T(8,128)(2,1)S(1)}, u32[]{:S(2)}, u32[]{:S(2)}) async-start(bf16[128,8,128]{2,1,0:T(8,128)(2,1)} %fusion.13), calls=%async_computation | async-start | bytes 524288 | tf_op jit(solution)/shard_map/all_to_all | solution.py:90
  206.4 4.1 %copy-start.2 = (bf16[4096,256]{1,0:T(8,128)(2,1)S(1)}, bf16[4096,256]{1,0:T(8,128)(2,1)}, u32[]{:S(2)}) copy-start(bf16[4096,256]{1,0:T(8,128)(2,1)} %all-gather.3.cloned.1.call-done) | copy-start | bytes 6291460
  206.4 4.1 %copy-start.3 = (bf16[4096,256]{1,0:T(8,128)(2,1)S(1)}, bf16[4096,256]{1,0:T(8,128)(2,1)}, u32[]{:S(2)}) copy-start(bf16[4096,256]{1,0:T(8,128)(2,1)} %all-gather.5.cloned.1.call-done) | copy-start | bytes 6291460
  326.0 72.8 %copy-start.1 = (bf16[768,128]{1,0:T(8,128)(2,1)S(1)}, bf16[768,128]{1,0:T(8,128)(2,1)}, u32[]{:S(2)}) copy-start(bf16[768,128]{1,0:T(8,128)(2,1)} %param.8) | copy-start | bytes 589828
Sparse Core Ops, SparseCore 0:
  32.9 77.0 reduce-scatter.1
  112.4 47.0 all-gather.2
  161.9 44.5 all-gather.4
where the time goes:
time: 406 us; the launch traced here: 405 us
  waiting for transfers between devices  110 us (27%)
  other arithmetic  75.1 us (18%)
  blocking collectives  72.2 us (18%)
  local copies, waits for them, and re-layouts  63 us (16%)
  matrix products  62.9 us (15%)
  between operations  14.1 us (3%)
  starting transfers between devices  8.09 us (2%)
    pmin x1, blocking collectives, local(): group_lowest = lax.pmin(partial_value, 'list')  72.2 us
    reduce_scatter x1, waiting for transfers between devices, local(): lax.psum_scatter(jnp.where(inside[:, None], picked.astype(jnp.float32), 0...  66.4 us
    dot_general x4, matrix products, sweep_block(): lax.dot_general(stacked, block, (((1,), (1,)), ((), ())), preferred_eleme...  61.2 us
    reduce_min x4, other arithmetic, sweep_block(): return jnp.minimum(lowest, jnp.min(scores, axis=1))  51.7 us
    all_gather x2, waiting for transfers between devices, local(): lax.all_gather((head_prefix, residual), 'list', axis=0, tiled=True)  43.5 us
    reshape x3, local copies, waits for them, and re-layouts, local(): all_ids = list_ids.reshape(device_count, -1)  25.5 us
    gather x1, local copies, waits for them, and re-layouts, local(): jnp.take(centroid_prefix, jnp.clip(local_index, 0, per_device - 1), axis=0)  16.9 us
    unnamed x13, local copies, waits for them, and re-layouts  8.37 us
  transfers between devices with their start and end apart: 4, of which 2 were waited for; matrix products, arithmetic and copies ran while one was open for 14% of the time, Pallas kernels for 0%

commit v1 on v0

v1 whole, which is shorter than its diff:
```python
import functools

import jax
import jax.numpy as jnp
from jax import lax
from jax.experimental import pallas as pl
from jax.experimental.pallas import tpu as pltpu
from jax.sharding import PartitionSpec as P

PREFIX = 256
N_DP = 8
N_LIST = 16
SIDE = 4
ROWS = 256
HALF = 128
LISTS = 4096
CAP = 8
SLOTS = N_DP * CAP
PDIM = 128

soar_weight = 1.5
masked_score = 1e30
NT = (((1,), (1,)), ((), ()))
bf16 = jnp.bfloat16
f32 = jnp.float32
i32 = jnp.int32


def iota(shape, dim):
    return lax.broadcasted_iota(i32, shape, dim)


def ones_where(mask):
    return jnp.where(mask, 1.0, 0.0)


def dot(a, b):
    return jnp.dot(a, b, preferred_element_type=f32)


def params(mib):
    return pltpu.CompilerParams(vmem_limit_bytes=mib << 20)


def split3(x):
    hi = x.astype(bf16)
    rest = x - hi.astype(f32)
    mid = rest.astype(bf16)
    low = (rest - mid.astype(f32)).astype(bf16)
    return hi, mid, low


def to_column(row, n):
    eye = iota((n, n), 0) == iota((n, n), 1)
    return jnp.sum(jnp.where(eye, jnp.broadcast_to(row, (n, n)), 0.0), axis=1, keepdims=True)


def to_row(column, n):
    eye = iota((n, n), 0) == iota((n, n), 1)
    return jnp.sum(jnp.where(eye, jnp.broadcast_to(column, (n, n)), 0.0), axis=0, keepdims=True)


def pack_kernel(place, ids_ref, c_ref, out_ref):
    list_place = place[1]
    ids = ids_ref[0]
    inside = (ids >> 12) == list_place
    upto = ones_where(iota((ROWS, ROWS), 0) <= iota((ROWS, ROWS), 1)).astype(bf16)
    count = dot(ones_where(inside).astype(bf16), upto)
    rank = jnp.where(inside, count - 1.0, -1.0)
    local = (ids & (LISTS - 1)).astype(f32) + 1.0
    slot = iota((SLOTS, ROWS), 0).astype(f32)
    lane = iota((4 * SLOTS, LISTS), 1).astype(f32)
    for g in range(N_LIST // 4):
        picks = []
        for s in range(4 * g, 4 * g + 4):
            hit = slot == rank[s : s + 1, :]
            picks.append(jnp.sum(jnp.where(hit, local[s : s + 1, :], 0.0), axis=1, keepdims=True))
        pick = jnp.concatenate(picks, axis=0) - 1.0
        hot = ones_where(lane == pick).astype(bf16)
        out_ref[4 * g : 4 * g + 4] = (
            dot(hot, c_ref[...]).astype(bf16).reshape(4, SLOTS, PREFIX)
        )


def pack(place, ids, centroids):
    return pl.pallas_call(
        pack_kernel,
        out_shape=jax.ShapeDtypeStruct((N_LIST, SLOTS, PREFIX), bf16),
        grid_spec=pltpu.PrefetchScalarGridSpec(
            num_scalar_prefetch=1,
            grid=(1,),
            in_specs=[
                pl.BlockSpec((1, N_LIST, ROWS), lambda i, p: (0, p[0], 0)),
                pl.BlockSpec((LISTS, PREFIX), lambda i, p: (0, 0)),
            ],
            out_specs=pl.BlockSpec((N_LIST, SLOTS, PREFIX), lambda i, p: (0, 0, 0)),
        ),
        compiler_params=params(40),
        name="pack_prefixes",
    )(place, ids, centroids)


def residual_kernel(place, ids_ref, got_ref, head_ref, resid_ref, square_ref):
    own = place[1]
    ids = ids_ref[0, pl.ds(own, 1), :]
    shard = ids >> 12
    member = iota((N_LIST, ROWS), 0) == shard
    upto = ones_where(iota((ROWS, ROWS), 0) <= iota((ROWS, ROWS), 1)).astype(bf16)
    count = dot(ones_where(member).astype(bf16), upto)
    rank = jnp.sum(jnp.where(member, count - 1.0, 0.0), axis=0, keepdims=True)
    slot = to_column((shard * SLOTS).astype(f32) + rank, ROWS)
    hot = ones_where(iota((ROWS, N_LIST * SLOTS), 1).astype(f32) == slot).astype(bf16)
    primary = dot(hot, got_ref[...].reshape(N_LIST * SLOTS, PREFIX))
    head = head_ref[...].astype(f32)
    resid = (head - primary).astype(bf16).astype(f32)
    power = jnp.sum(resid * resid, axis=1, keepdims=True) * (1.0 / PREFIX) + 1e-6
    scale = jnp.sqrt(soar_weight / (PREFIX * power))
    resid_ref[...] = (resid * scale).astype(bf16)
    square_ref[...] = to_row(jnp.sum(head * head, axis=1, keepdims=True), ROWS)


def residuals(place, ids, got, vectors):
    return pl.pallas_call(
        residual_kernel,
        out_shape=(
            jax.ShapeDtypeStruct((ROWS, PREFIX), bf16),
            jax.ShapeDtypeStruct((1, ROWS), f32),
        ),
        grid_spec=pltpu.PrefetchScalarGridSpec(
            num_scalar_prefetch=1,
            grid=(1,),
            in_specs=[
                pl.BlockSpec((1, N_LIST, ROWS), lambda i, p: (0, p[0], 0)),
                pl.BlockSpec((N_LIST, SLOTS, PREFIX), lambda i, p: (0, 0, 0)),
                pl.BlockSpec((ROWS, PREFIX), lambda i, p: (0, 0)),
            ],
            out_specs=(
                pl.BlockSpec((ROWS, PREFIX), lambda i, p: (0, 0)),
                pl.BlockSpec((1, ROWS), lambda i, p: (0, 0)),
            ),
        ),
        compiler_params=params(32),
        name="own_residuals",
    )(place, ids, got, vectors)


def owned_kernel(place, c_ref, proj_ref, hi_ref, mid_ref, low_ref, square_ref):
    mine = place[0]
    c = c_ref[...]
    rows = c.shape[0]
    full = dot(c, proj_ref[...]).reshape(rows // N_DP, N_DP, PDIM)
    keep = iota((rows // N_DP, N_DP, PDIM), 1) == mine
    owned = jnp.sum(jnp.where(keep, full, 0.0), axis=1)
    hi_ref[...], mid_ref[...], low_ref[...] = split3(owned)
    head = c[:, :PREFIX].astype(f32)
    square = head * head
    upper = square.astype(bf16)
    lower = (square - upper.astype(f32)).astype(bf16)
    one = jnp.ones((PREFIX, 128), bf16)
    square_ref[...] = dot(upper, one) + dot(lower, one)


def owned(place, centroids, projection):
    block = 1024
    part = jax.ShapeDtypeStruct((LISTS // N_DP, PDIM), bf16)
    part_spec = pl.BlockSpec((block // N_DP, PDIM), lambda i, p: (i, 0))
    return pl.pallas_call(
        owned_kernel,
        out_shape=(part, part, part, jax.ShapeDtypeStruct((LISTS, 128), f32)),
        grid_spec=pltpu.PrefetchScalarGridSpec(
            num_scalar_prefetch=1,
            grid=(LISTS // block,),
            in_specs=[
                pl.BlockSpec((block, centroids.shape[1]), lambda i, p: (i, 0)),
                pl.BlockSpec(projection.shape, lambda i, p: (0, 0)),
            ],
            out_specs=(
                part_spec,
                part_spec,
                part_spec,
                pl.BlockSpec((block, 128), lambda i, p: (i, 0)),
            ),
        ),
        compiler_params=params(32),
        name="owned_projection",
    )(place, centroids, projection)


def rank_tables(first, second):
    before = ones_where(iota((ROWS, ROWS), 0) < iota((ROWS, ROWS), 1)).astype(bf16)
    one0, one1 = ones_where(first), ones_where(second)
    earlier = dot((one0 + one1).astype(bf16), before)
    return jnp.where(first, earlier, -1.0), jnp.where(second, earlier + one0, -1.0)


def eightfold(table):
    n = table.shape[0]
    return jnp.broadcast_to(table[:, None, :], (n, CAP, ROWS)).reshape(n * CAP, ROWS)


def send_kernel(place, id0_ref, id1_ref, vec_ref, proj_ref, out_ref):
    own = place[1]
    devices = N_DP * N_LIST
    hits = []
    for ref in (id0_ref, id1_ref):
        ids = ref[0, pl.ds(own, 1), :]
        hits.append(iota((devices, ROWS), 0) == (ids & (N_DP - 1)) * N_LIST + (ids >> 12))
    rank0, rank1 = rank_tables(*hits)
    slot = (iota((devices * CAP, ROWS), 0) & (CAP - 1)).astype(f32)
    hot = ones_where((eightfold(rank0) == slot) | (eightfold(rank1) == slot)).astype(bf16)
    payload = dot(vec_ref[...], proj_ref[...]).astype(bf16)
    out_ref[...] = dot(hot, payload).astype(bf16).reshape(devices, CAP, PDIM)


def outgoing(place, ids, vectors, projection):
    devices = N_DP * N_LIST
    return pl.pallas_call(
        send_kernel,
        out_shape=jax.ShapeDtypeStruct((devices, CAP, PDIM), bf16),
        grid_spec=pltpu.PrefetchScalarGridSpec(
            num_scalar_prefetch=1,
            grid=(1,),
            in_specs=[
                pl.BlockSpec((1, N_LIST, ROWS), lambda i, p: (0, p[0], 0)),
                pl.BlockSpec((1, N_LIST, ROWS), lambda i, p: (1, p[0], 0)),
                pl.BlockSpec(vectors.shape, lambda i, p: (0, 0)),
                pl.BlockSpec(projection.shape, lambda i, p: (0, 0)),
            ],
            out_specs=pl.BlockSpec((devices, CAP, PDIM), lambda i, p: (0, 0, 0)),
        ),
        compiler_params=params(32),
        name="outgoing_rows",
    )(place, ids, ids, vectors, projection)


def place_kernel(place, ids_ref, got_ref, hi_ref, mid_ref, low_ref, out_ref):
    devices = N_DP * N_LIST
    id0, id1 = ids_ref[0], ids_ref[1]
    hits, local = [], []
    for ids in (id0, id1):
        hits.append(((ids & (N_DP - 1)) == place[0]) & ((ids >> 12) == place[1]))
        local.append(((ids & (LISTS - 1)) >> 3).astype(f32) + 1.0)
    rank0, rank1 = rank_tables(*hits)
    slot = (iota((devices * CAP, ROWS), 0) & (CAP - 1)).astype(f32)
    pick = jnp.where(eightfold(rank0) == slot, eightfold(local[0]), 0.0)
    pick += jnp.where(eightfold(rank1) == slot, eightfold(local[1]), 0.0)
    pick = jnp.sum(pick, axis=1, keepdims=True) - 1.0
    per_owner = LISTS // N_DP
    hot = ones_where(iota((devices * CAP, per_owner), 1).astype(f32) == pick).astype(bf16)
    centroid = dot(hot, hi_ref[...]) + dot(hot, mid_ref[...]) + dot(hot, low_ref[...])
    got = got_ref[...].reshape(devices * CAP, PDIM).astype(f32)
    out_ref[...] = jnp.where(pick >= 0.0, got - centroid, 0.0).astype(bf16)


def placement(place, ids, got, parts):
    devices = N_DP * N_LIST
    part_spec = pl.BlockSpec(parts[0].shape, lambda i, p: (0, 0))
    return pl.pallas_call(
        place_kernel,
        out_shape=jax.ShapeDtypeStruct((devices * CAP, PDIM), bf16),
        grid_spec=pltpu.PrefetchScalarGridSpec(
            num_scalar_prefetch=1,
            grid=(1,),
            in_specs=[
                pl.BlockSpec(ids.shape, lambda i, p: (0, 0, 0)),
                pl.BlockSpec(got.shape, lambda i, p: (0, 0, 0)),
                part_spec,
                part_spec,
                part_spec,
            ],
            out_specs=pl.BlockSpec((devices * CAP, PDIM), lambda i, p: (0, 0)),
        ),
        compiler_params=params(32),
        name="place_rows",
    )(place, ids, got, *parts)


def score_kernel(halves, n_arrays, has_last, place, *refs):
    ids_ref, c_hbm, square_hbm = refs[:3]
    arrays = refs[3 : 3 + n_arrays]
    rest = refs[3 + n_arrays :]
    last_ref = rest[0] if has_last else None
    out_ref, c_ref, square_ref, head_ref, resid_ref, prim_ref, low_ref, sems = rest[has_last:]
    tiles = len(halves) // 2
    own = place[1]
    copies = [
        pltpu.make_async_copy(c_hbm.at[:, pl.ds(0, PREFIX)], c_ref, sems.at[0]),
        pltpu.make_async_copy(square_hbm, square_ref, sems.at[1]),
    ]
    sources = []
    for n, (h_at, h_row, r_at, r_row, dy, dz, half) in enumerate(halves):
        to = pl.ds(n * HALF, HALF)
        copies.append(
            pltpu.make_async_copy(
                arrays[h_at].at[pl.ds(h_row, HALF), pl.ds(0, PREFIX)], head_ref.at[to], sems.at[2 + 2 * n]
            )
        )
        copies.append(
            pltpu.make_async_copy(
                arrays[r_at].at[pl.ds(r_row, HALF), pl.ds(0, PREFIX)], resid_ref.at[to], sems.at[3 + 2 * n]
            )
        )
        y = (own // SIDE + SIDE - dy) % SIDE
        z = (own % SIDE + SIDE - dz) % SIDE
        sources.append(y * SIDE + z)
    for copy in copies:
        copy.start()
    for n, half in enumerate(halves):
        row = ids_ref[0, pl.ds(sources[n], 1), :] - own * LISTS
        prim_ref[n // 2 : n // 2 + 1, (n % 2) * HALF : (n % 2 + 1) * HALF] = row[
            :, half[6] * HALF : (half[6] + 1) * HALF
        ]
    for copy in copies:
        copy.wait()
    eye = iota((ROWS, ROWS), 0) == iota((ROWS, ROWS), 1)
    number = iota((LISTS, ROWS), 0)

    def one_tile(tile, carry):
        at = pl.multiple_of(tile * ROWS, ROWS)
        head = head_ref[pl.ds(at, ROWS), :]
        resid = resid_ref[pl.ds(at, ROWS), :]
        both = lax.dot_general(head, resid, NT, preferred_element_type=f32)
        cross = jnp.sum(jnp.where(eye, both, 0.0), axis=0, keepdims=True)
        dot_head = lax.dot_general(c_ref[...], head * bf16(-2), NT, preferred_element_type=f32)
        dot_resid = lax.dot_general(c_ref[...], resid, NT, preferred_element_type=f32)
        square = square_ref[...]
        square = jnp.concatenate([square, square], axis=1)
        along = cross - dot_resid
        score = (dot_head + square) + along * along
        score = jnp.where(number == prim_ref[pl.ds(tile, 1), :], masked_score, score)
        low_ref[pl.ds(tile, 1), :] = jnp.min(
            jnp.min(score.reshape(LISTS // 8, 8, ROWS), axis=0), axis=0, keepdims=True
        )
        return carry

    lax.fori_loop(0, tiles, one_tile, 0, unroll=2)
    result = last_ref[...] if has_last else jnp.zeros(out_ref.shape, f32)
    row = iota(result.shape, 0)
    side = iota(result.shape, 1) // HALF
    for n, half in enumerate(halves):
        low = low_ref[n // 2 : n // 2 + 1, (n % 2) * HALF : (n % 2 + 1) * HALF]
        low = jnp.broadcast_to(jnp.concatenate([low, low], axis=1), result.shape)
        result = jnp.where((row == sources[n]) & (side == half[6]), low, result)
    out_ref[...] = result


def scores(name, place, ids, centroids, square, arrays, halves, last=None):
    rows = len(halves) * HALF
    has_last = last is not None
    low_spec = pl.BlockSpec((N_LIST, ROWS), lambda i, p: (0, 0))
    return pl.pallas_call(
        functools.partial(score_kernel, halves, len(arrays), has_last),
        out_shape=jax.ShapeDtypeStruct((N_LIST, ROWS), f32),
        grid_spec=pltpu.PrefetchScalarGridSpec(
            num_scalar_prefetch=1,
            grid=(1,),
            in_specs=[pl.BlockSpec((1, N_LIST, ROWS), lambda i, p: (0, p[0], 0))]
            + [pl.BlockSpec(memory_space=pl.ANY)] * (2 + len(arrays))
            + [low_spec] * has_last,
            out_specs=low_spec,
            scratch_shapes=[
                pltpu.VMEM((LISTS, PREFIX), bf16),
                pltpu.VMEM((LISTS, 128), f32),
                pltpu.VMEM((rows, PREFIX), bf16),
                pltpu.VMEM((rows, PREFIX), bf16),
                pltpu.VMEM((max(8, rows // ROWS), ROWS), i32),
                pltpu.VMEM((max(8, rows // ROWS), ROWS), f32),
                pltpu.SemaphoreType.DMA((2 + 2 * len(halves),)),
            ],
        ),
        compiler_params=params(40),
        name=name,
    )(place, ids, centroids, square, *arrays, *([last] if has_last else []))


def final_kernel(got_ref, square_ref, out_ref):
    low = jnp.min(got_ref[...], axis=0, keepdims=True)
    out_ref[...] = (low + square_ref[...]) * (1.0 / PREFIX)


def step(dy, dz):
    pairs = []
    for at in range(N_LIST):
        y, z = divmod(at, SIDE)
        pairs.append((at, (y + dy) % SIDE * SIDE + (z + dz) % SIDE))
    return pairs


def shift(x, dy, dz):
    return lax.ppermute(x, "list", step(dy, dz))


def local(vectors, centroids, projection, list_ids):
    place = jnp.stack([lax.axis_index("dp"), lax.axis_index("list")]).astype(i32)
    ids = list_ids.T.reshape(2, N_DP * N_LIST, ROWS)
    head = vectors[:, :PREFIX]

    head_z = [head] + [shift(head, 0, dz) for dz in range(1, SIDE)]
    head_row = jnp.concatenate(head_z, axis=0)
    head_y = [None] + [shift(head_row, dy, 0) for dy in range(1, SIDE)]

    slots = pack(place, ids, centroids)
    got = lax.all_to_all(slots, "list", 0, 0, tiled=True)
    resid, head_square = residuals(place, ids, got, vectors)

    low, high = resid[:HALF], resid[HALF:]
    low_z = [low] + [shift(low, 0, dz) for dz in range(1, SIDE)]
    high_y = [high] + [shift(high, dy, 0) for dy in range(1, SIDE)]
    low_row = jnp.concatenate(low_z, axis=0)
    high_column = jnp.concatenate(high_y, axis=0)
    low_zy = [None] + [shift(low_row, dy, 0) for dy in range(1, SIDE)]
    high_yz = [None] + [shift(high_column, 0, dz) for dz in range(1, SIDE)]

    rows_out = outgoing(place, ids, vectors, projection)
    rows_in = lax.all_to_all(rows_out, ("dp", "list"), 0, 0, tiled=True)
    *parts, square = owned(place, centroids, projection)
    placed = placement(place, ids, rows_in, parts)

    arrays = [vectors, *head_z[1:], *head_y[1:]]

    def head_of(dy, dz, half):
        if dy == 0:
            return dz, half * HALF
        return SIDE - 1 + dy, dz * ROWS + half * HALF

    def call(name, given, blocks, last=None):
        used, halves = [], []
        for r_array, r_row, dy, dz, half in blocks:
            h_at, h_row = head_of(dy, dz, half)
            spots = []
            for x in (arrays[h_at], r_array):
                known = [n for n, y in enumerate(used) if y is x]
                if not known:
                    used.append(x)
                    known = [len(used) - 1]
                spots.append(known[0])
            halves.append((spots[0], h_row, spots[1], r_row, dy, dz, half))
        return scores(name, place, ids, centroids, square, used, tuple(halves), last)

    near = [(low, 0, 0, 0, 0), (high, 0, 0, 0, 1)]
    near += [(low_z[dz], 0, 0, dz, 0) for dz in range(1, SIDE)]
    near += [(high_y[dy], 0, dy, 0, 1) for dy in range(1, SIDE)]

    def far(d):
        blocks = [(low_zy[d], dz * HALF, d, dz, 0) for dz in range(SIDE)]
        return blocks + [(high_yz[d], dy * HALF, dy, d, 1) for dy in range(SIDE)]

    lowest = call("scores_near", arrays, near)
    lowest = call("scores_next", arrays, far(1) + far(3), lowest)
    lowest = call("scores_far", arrays, far(2), lowest)
    back = lax.all_to_all(lowest, "list", 0, 0, tiled=True)
    lowest_score = pl.pallas_call(
        final_kernel, out_shape=jax.ShapeDtypeStruct((1, ROWS), f32), name="lowest"
    )(back, head_square)
    return placed, lowest_score.reshape(ROWS)


def solution(mesh):
    return jax.shard_map(
        local,
        mesh=mesh,
        in_specs=(P(("dp", "list"), None), P("list", None), P(), P()),
        out_specs=(P(("dp", "list"), None), P(("dp", "list"))),
        check_vma=False,
    )
```

time: 406 us -> 146 us (0.36)
  other arithmetic: 75.1 us -> 2.35 us
  blocking collectives: 72.2 us -> 0 us
  waiting for transfers between devices: 110 us -> 41.1 us
  matrix products: 62.9 us -> 0 us
  local copies, waits for them, and re-layouts: 63 us -> 10.5 us
  Pallas kernels: 0 us -> 44.3 us
  starting transfers between devices: 8.09 us -> 46.4 us
  between operations: 14.1 us -> 0.88 us
    pmin x1 -> x0, blocking collectives: 72.2 us -> none  [local(): group_lowest = lax.pmin(partial_value, 'list')]
    reduce_scatter x1 -> x0, waiting for transfers between devices: 66.4 us -> none  [local(): lax.psum_scatter(jnp.where(inside[:, None], picked.astype(jnp.float32), 0...]
    dot_general x6 -> x0, matrix products: 62.9 us -> none  [the longest x4 61.2 us: sweep_block(): lax.dot_general(stacked, block, (((1,), (1,)), ((), ())), preferred_eleme...]
    reduce_min x4 -> x0, other arithmetic: 51.7 us -> none  [sweep_block(): return jnp.minimum(lowest, jnp.min(scores, axis=1))]
    pallas_call x0 -> x9, Pallas kernels: none -> 44.3 us  [the longest x3 28.7 us: scores(): pl.pallas_call(functools.partial(score_kernel, halves, len(arrays), has_l...]
    all_gather x2 -> x0, waiting for transfers between devices: 43.5 us -> none  [local(): lax.all_gather((head_prefix, residual), 'list', axis=0, tiled=True)]
    ppermute x0 -> x18, waiting for transfers between devices: none -> 36.3 us  [shift(): return lax.ppermute(x, 'list', step(dy, dz))]
    reshape x5 -> x0, local copies, waits for them, and re-layouts: 25.8 us -> none  [the longest x3 25.5 us: local(): all_ids = list_ids.reshape(device_count, -1)]
  transfers between devices with their start and end apart: 4 -> 21, of which waited for: 2 -> 8; matrix products, arithmetic and copies ran while one was open for 14% -> 2% of each run, Pallas kernels for 0% -> 27%
where the time goes in v1:
time: 146 us
  starting transfers between devices  46.4 us (32%)
  Pallas kernels  44.3 us (30%)
  waiting for transfers between devices  41.1 us (28%)
  local copies, waits for them, and re-layouts  10.5 us (7%)
  other arithmetic  2.35 us (2%)
    ppermute x18, waiting for transfers between devices, shift(): return lax.ppermute(x, 'list', step(dy, dz))  36.3 us
    pallas_call x3, Pallas kernels, scores(): pl.pallas_call(functools.partial(score_kernel, halves, len(arrays), has_l...  28.7 us
    ppermute x18, starting transfers between devices, shift(): return lax.ppermute(x, 'list', step(dy, dz))  21.4 us
    all_to_all x1, starting transfers between devices, local(): rows_in = lax.all_to_all(rows_out, ('dp', 'list'), 0, 0, tiled=True)  10.2 us
    unnamed x34, local copies, waits for them, and re-layouts  9.89 us
    all_to_all x1, starting transfers between devices, local(): got = lax.all_to_all(slots, 'list', 0, 0, tiled=True)  8.13 us
    all_to_all x1, starting transfers between devices, local(): back = lax.all_to_all(lowest, 'list', 0, 0, tiled=True)  6.6 us
    all_to_all x1, waiting for transfers between devices, local(): back = lax.all_to_all(lowest, 'list', 0, 0, tiled=True)  4.7 us
  transfers between devices with their start and end apart: 21, of which 8 were waited for; matrix products, arithmetic and copies ran while one was open for 2% of the time, Pallas kernels for 27%

profile of v1, /device:TPU:0, one launch (start us, length us, event | category | flops | bytes accessed | tf_op | source)
XLA Modules:
  0.0 145.5 jit_solution(952548215450310671)
XLA Ops:
  0.6 1.0 copy.11
  1.7 2.8 %copy-done = bf16[4096,768]{1,0:T(8,128)(2,1)S(1)} copy-done((bf16[4096,768]{1,0:T(8,128)(2,1)S(1)}, bf16[4096,768]{1,0:T(8,128)(2,1)}, u32[]{:S(2)}) %copy-start) | copy-done | bytes 6291480
  4.5 4.1 %pack_prefixes.1 = bf16[16,64,256]{2,1,0:T(8,128)(2,1)} custom-call(s32[2]{0:T(128)S(1)} %pad_add_fusion.place, s32[2,128,256]{2,1,0:T(8,128)S(1)} %bitcast.12, bf16[4096,768]{1,0:T(8,128)(2,1)S(1)} %copy-done), custom_call_target="tpu_custom_call" | custom-call | tf_op jit(solution)/shard_map/pack_prefixes/pallas_call | solution.py:86
  8.6 8.1 %all-to-all-start.1 = ((bf16[16,64,256]{2,1,0:T(8,128)(2,1)}), bf16[16,64,256]{2,1,0:T(8,128)(2,1)S(1)}, u32[]{:S(2)}, u32[]{:S(2)}) async-start(bf16[16,64,256]{2,1,0:T(8,128)(2,1)} %pack_prefixes.1), calls=%async_computation.1 | async-start | bytes 1048576 | tf_op jit(solution)/shard_map/all_to_all | solution.py:403
  16.8 2.0 %collective-permute-start = (bf16[256,256]{1,0:T(8,128)(2,1)S(1)}, bf16[256,256]{1,0:T(8,128)(2,1)S(1)}, u32[]{:S(2)}, u32[]{:S(2)}) collective-permute-start(bf16[256,256]{1,0:T(8,128)(2,1)S(1)} %slice.9), channel_id=1, source_target_pairs={{0,1},{1,2},{2,3},{3,0},{4,5},{5,6},{6,7},{7,4},{8,9},{9,10},{10,1... | collective-permute-start | bytes 393224 | tf_op jit(solution)/shard_map/ppermute | solution.py:390
  18.8 2.7 %collective-permute-start.1 = (bf16[256,256]{1,0:T(8,128)(2,1)S(1)}, bf16[256,256]{1,0:T(8,128)(2,1)S(1)}, u32[]{:S(2)}, u32[]{:S(2)}) collective-permute-start(bf16[256,256]{1,0:T(8,128)(2,1)S(1)} %slice.9), channel_id=1, source_target_pairs={{0,2},{1,3},{2,0},{3,1},{4,6},{5,7},{6,4},{7,5},{8,10},{9,11},{10,... | collective-permute-start | bytes 393224 | tf_op jit(solution)/shard_map/ppermute | solution.py:390
  21.5 1.5 %collective-permute-start.2 = (bf16[256,256]{1,0:T(8,128)(2,1)S(1)}, bf16[256,256]{1,0:T(8,128)(2,1)S(1)}, u32[]{:S(2)}, u32[]{:S(2)}) collective-permute-start(bf16[256,256]{1,0:T(8,128)(2,1)S(1)} %slice.9), channel_id=1, source_target_pairs={{0,3},{1,0},{2,1},{3,2},{4,7},{5,4},{6,5},{7,6},{8,11},{9,8},{10,9... | collective-permute-start | bytes 393224 | tf_op jit(solution)/shard_map/ppermute | solution.py:390
  22.9 6.7 %collective-permute-done.refs_6_.refs_5_ = bf16[256,256]{1,0:T(8,128)(2,1)S(1)} collective-permute-done((bf16[256,256]{1,0:T(8,128)(2,1)S(1)}, bf16[256,256]{1,0:T(8,128)(2,1)S(1)}, u32[]{:S(2)}, u32[]{:S(2)}) %collective-permute-start) | collective-permute-done | bytes 131104 | tf_op jit(solution)/shard_map/ppermute | solution.py:390
  29.6 2.3 %collective-permute-done.1.refs_8_.refs_5_ = bf16[256,256]{1,0:T(8,128)(2,1)S(1)} collective-permute-done((bf16[256,256]{1,0:T(8,128)(2,1)S(1)}, bf16[256,256]{1,0:T(8,128)(2,1)S(1)}, u32[]{:S(2)}, u32[]{:S(2)}) %collective-permute-start.1) | collective-permute-done | bytes 131104 | tf_op jit(solution)/shard_map/ppermute | solution.py:390
  31.8 0.8 pad_maximum_fusion
  32.7 1.5 %collective-permute-start.12 = (bf16[1024,256]{1,0:T(8,128)(2,1)}, bf16[1024,256]{1,0:T(8,128)(2,1)S(1)}, u32[]{:S(2)}, u32[]{:S(2)}) collective-permute-start(bf16[1024,256]{1,0:T(8,128)(2,1)} %pad_maximum_fusion), channel_id=1, source_target_pairs={{0,4},{1,5},{2,6},{3,7},{4,8},{5,9},{6,10},{7,11},{8,12},{9,13},{1... | collective-permute-start | bytes 1572872 | tf_op jit(solution)/shard_map/ppermute | solution.py:390
  34.1 1.8 %collective-permute-start.13 = (bf16[1024,256]{1,0:T(8,128)(2,1)}, bf16[1024,256]{1,0:T(8,128)(2,1)S(1)}, u32[]{:S(2)}, u32[]{:S(2)}) collective-permute-start(bf16[1024,256]{1,0:T(8,128)(2,1)} %pad_maximum_fusion), channel_id=1, source_target_pairs={{0,12},{1,13},{2,14},{3,15},{4,0},{5,1},{6,2},{7,3},{8,4},{9,5},{1... | collective-permute-start | bytes 1572872 | tf_op jit(solution)/shard_map/ppermute | solution.py:390
  35.9 1.7 %collective-permute-start.3 = (bf16[1024,256]{1,0:T(8,128)(2,1)}, bf16[1024,256]{1,0:T(8,128)(2,1)S(1)}, u32[]{:S(2)}, u32[]{:S(2)}) collective-permute-start(bf16[1024,256]{1,0:T(8,128)(2,1)} %pad_maximum_fusion), channel_id=1, source_target_pairs={{0,8},{1,9},{2,10},{3,11},{4,12},{5,13},{6,14},{7,15},{8,0},{9,1},... | collective-permute-start | bytes 1572872 | tf_op jit(solution)/shard_map/ppermute | solution.py:390
  37.6 1.2 own_residuals.1
  38.8 0.3 collective-permute-start.4
  39.1 2.4 %collective-permute-start.5 = (bf16[128,256]{1,0:T(8,128)(2,1)S(1)}, bf16[128,256]{1,0:T(8,128)(2,1)S(1)}, u32[]{:S(2)}, u32[]{:S(2)}) collective-permute-start(bf16[128,256]{1,0:T(8,128)(2,1)S(1)} %get-tuple-element.15.refs_4_), channel_id=1, source_target_pairs={{0,2},{1,3},{2,0},{3,1},{4,6},{5,7},{6,4},{7,5},{8,10},{9,11},{10,... | collective-permute-start | bytes 196616 | tf_op jit(solution)/shard_map/ppermute | solution.py:390
  41.5 3.5 %collective-permute-done.4.refs_7_ = bf16[128,256]{1,0:T(8,128)(2,1)S(1)} collective-permute-done((bf16[128,256]{1,0:T(8,128)(2,1)S(1)}, bf16[128,256]{1,0:T(8,128)(2,1)S(1)}, u32[]{:S(2)}, u32[]{:S(2)}) %collective-permute-start.4) | collective-permute-done | bytes 65568 | tf_op jit(solution)/shard_map/ppermute | solution.py:390
  45.1 1.2 collective-permute-start.10
  46.3 3.0 %collective-permute-done.6.refs_11_ = bf16[128,256]{1,0:T(8,128)(2,1)S(1)} collective-permute-done((bf16[128,256]{1,0:T(8,128)(2,1)S(1)}, bf16[128,256]{1,0:T(8,128)(2,1)S(1)}, u32[]{:S(2)}, u32[]{:S(2)}) %collective-permute-start.6) | collective-permute-done | bytes 65568 | tf_op jit(solution)/shard_map/ppermute | solution.py:390
  49.3 0.7 pad_maximum_fusion.1
  50.0 0.6 collective-permute-start.14
  50.6 9.1 %collective-permute-done.10.refs_17_ = bf16[128,256]{1,0:T(8,128)(2,1)S(1)} collective-permute-done((bf16[128,256]{1,0:T(8,128)(2,1)S(1)}, bf16[128,256]{1,0:T(8,128)(2,1)S(1)}, u32[]{:S(2)}, u32[]{:S(2)}) %collective-permute-start.10) | collective-permute-done | bytes 65568 | tf_op jit(solution)/shard_map/ppermute | solution.py:390
  59.7 6.6 %collective-permute-done.8.refs_13_ = bf16[128,256]{1,0:T(8,128)(2,1)S(1)} collective-permute-done((bf16[128,256]{1,0:T(8,128)(2,1)S(1)}, bf16[128,256]{1,0:T(8,128)(2,1)S(1)}, u32[]{:S(2)}, u32[]{:S(2)}) %collective-permute-start.8) | collective-permute-done | bytes 65568 | tf_op jit(solution)/shard_map/ppermute | solution.py:390
  66.3 0.6 collective-permute-start.9
  67.0 5.1 %collective-permute-done.9.refs_15_ = bf16[128,256]{1,0:T(8,128)(2,1)S(1)} collective-permute-done((bf16[128,256]{1,0:T(8,128)(2,1)S(1)}, bf16[128,256]{1,0:T(8,128)(2,1)S(1)}, u32[]{:S(2)}, u32[]{:S(2)}) %collective-permute-start.9) | collective-permute-done | bytes 65568 | tf_op jit(solution)/shard_map/ppermute | solution.py:390
  72.1 0.6 collective-permute-start.16
  72.7 0.7 pad_maximum_fusion.2
  73.4 1.7 %collective-permute-start.15 = (bf16[512,256]{1,0:T(8,128)(2,1)}, bf16[512,256]{1,0:T(8,128)(2,1)}, u32[]{:S(2)}, u32[]{:S(2)}) collective-permute-start(bf16[512,256]{1,0:T(8,128)(2,1)} %pad_maximum_fusion.2), channel_id=1, source_target_pairs={{0,1},{1,2},{2,3},{3,0},{4,5},{5,6},{6,7},{7,4},{8,9},{9,10},{10,1... | collective-permute-start | bytes 786440 | tf_op jit(solution)/shard_map/ppermute | solution.py:390
  75.1 1.5 %collective-permute-start.17 = (bf16[512,256]{1,0:T(8,128)(2,1)}, bf16[512,256]{1,0:T(8,128)(2,1)}, u32[]{:S(2)}, u32[]{:S(2)}) collective-permute-start(bf16[512,256]{1,0:T(8,128)(2,1)} %pad_maximum_fusion.2), channel_id=1, source_target_pairs={{0,3},{1,0},{2,1},{3,2},{4,7},{5,4},{6,5},{7,6},{8,11},{9,8},{10,9... | collective-permute-start | bytes 786440 | tf_op jit(solution)/shard_map/ppermute | solution.py:390
  76.7 1.2 collective-permute-start.11
  77.9 0.7 copy-done.7
  78.6 0.2 collective-permute-start.7
  78.8 1.9 %outgoing_rows.1 = bf16[128,8,128]{2,1,0:T(8,128)(2,1)} custom-call(s32[2]{0:T(128)S(1)} %pad_add_fusion.place, s32[2,128,256]{2,1,0:T(8,128)S(1)} %bitcast.14, s32[2,128,256]{2,1,0:T(8,128)S(1)} %bitcast.15, bf16[256,768]{1,0:T(8,128)(2,1)S(1)} %copy-done.3, bf16[768,128]{1,0:T(8,128)(2,1)S(1)} %copy-done.4), custom_call_target="tpu_custom_call" | custom-call | tf_op jit(solution)/shard_map/outgoing_rows/pallas_call | solution.py:217
  80.7 10.2 %all-to-all-start = ((bf16[128,8,128]{2,1,0:T(8,128)(2,1)}), bf16[128,8,128]{2,1,0:T(8,128)(2,1)S(1)}, u32[]{:S(2)}, u32[]{:S(2)}) async-start(bf16[128,8,128]{2,1,0:T(8,128)(2,1)} %outgoing_rows.1), calls=%async_computation | async-start | bytes 524288 | tf_op jit(solution)/shard_map/all_to_all | solution.py:415
  90.9 2.8 %copy-done.1 = bf16[4096,768]{1,0:T(8,128)(2,1)S(1)} copy-done((bf16[4096,768]{1,0:T(8,128)(2,1)S(1)}, bf16[4096,768]{1,0:T(8,128)(2,1)}, u32[]{:S(2)}) %copy-start.1) | copy-done | bytes 6291480
  93.7 4.3 %owned_projection.1 = (bf16[512,128]{1,0:T(8,128)(2,1)S(1)}, bf16[512,128]{1,0:T(8,128)(2,1)S(1)}, bf16[512,128]{1,0:T(8,128)(2,1)S(1)}, f32[4096,128]{1,0:T(8,128)S(1)}) custom-call(s32[2]{0:T(128)S(1)} %pad_add_fusion.place, bf16[4096,768]{1,0:T(8,128)(2,1)S(1)} %copy-done.1, bf16[768,128]{1,0:T(8,128)(2,1)S(1)} %copy-done.4), custom_call_target="tpu_custom_call" | custom-call | tf_op jit(solution)/shard_map/owned_projection/pallas_call | solution.py:167
  98.0 0.6 copy-done.9
  98.7 0.6 copy-done.11
  99.3 0.7 copy-done.13
  100.0 7.3 %scores_near.1.refs_12_ = f32[16,256]{1,0:T(8,128)S(1)} custom-call(s32[2]{0:T(128)S(1)} %pad_add_fusion.place, s32[2,128,256]{2,1,0:T(8,128)S(1)} %bitcast.16, bf16[4096,768]{1,0:T(8,128)(2,1)S(1)} %copy-done.2, f32[4096,128]{1,0:T(8,128)S(1)} %get-tuple-element.11.refs_2_, bf16[256,768]{1,0:T(8,128)(2,1)S(1)} %copy-done.3, ...), custom_call_target="tpu_custom_call" | custom-call | tf_op jit(solution)/shard_map/scores_near/pallas_call | solution.py:351
  107.4 13.8 %scores_next.1.refs_9_ = f32[16,256]{1,0:T(8,128)S(1)} custom-call(s32[2]{0:T(128)S(1)} %pad_add_fusion.place, s32[2,128,256]{2,1,0:T(8,128)S(1)} %bitcast.17, bf16[4096,768]{1,0:T(8,128)(2,1)S(1)} %copy-done.2, f32[4096,128]{1,0:T(8,128)S(1)} %get-tuple-element.11.refs_2_, bf16[1024,256]{1,0:T(8,128)(2,1)S(1)} %collective-permute-done.12.refs_12_.refs_3_.refs_7_, ...), custom_call_target="tpu_custom_call" | custom-call | tf_op jit(solution)/shard_map/scores_next/pallas_call | solution.py:351
  121.2 7.6 %scores_far.1 = f32[16,256]{1,0:T(8,128)S(1)} custom-call(s32[2]{0:T(128)S(1)} %pad_add_fusion.place, s32[2,128,256]{2,1,0:T(8,128)S(1)} %bitcast.18, bf16[4096,768]{1,0:T(8,128)(2,1)S(1)} %copy-done.2, f32[4096,128]{1,0:T(8,128)S(1)} %get-tuple-element.11.refs_2_, bf16[1024,256]{1,0:T(8,128)(2,1)S(1)} %collective-permute-done.3.refs_14_.refs_7_.refs_3_, ...), custom_call_target="tpu_custom_call" | custom-call | tf_op jit(solution)/shard_map/scores_far/pallas_call | solution.py:351
  128.8 0.6 copy.6
  129.4 6.6 %all-to-all-start.2 = ((f32[16,1,256]{2,1,0:T(1,128)}), f32[16,1,256]{2,1,0:T(1,128)S(1)}, u32[]{:S(2)}, u32[]{:S(2)}) async-start(f32[16,1,256]{2,1,0:T(1,128)} %copy.6), calls=%async_computation.2 | async-start | bytes 32768 | tf_op jit(solution)/shard_map/all_to_all | solution.py:451
  136.1 2.9 %place_rows.1 = bf16[1024,128]{1,0:T(8,128)(2,1)} custom-call(s32[2]{0:T(128)S(1)} %pad_add_fusion.place, s32[2,128,256]{2,1,0:T(8,128)S(1)} %bitcast.19, bf16[128,8,128]{2,1,0:T(8,128)(2,1)S(1)} %all-to-all-done.got_ref, bf16[512,128]{1,0:T(8,128)(2,1)S(1)} %copy-done.10, bf16[512,128]{1,0:T(8,128)(2,1)S(1)} %copy-done.12, bf16[512,128]{1,0:T(8,128)(2,1)S(1)} %copy-done.14), custom_call_target="tpu_custom_call" | custom-call | tf_op jit(solution)/shard_map/place_rows/pallas_call | solution.py:258
  138.9 4.7 %all-to-all-done.2 = f32[16,1,256]{2,1,0:T(1,128)S(1)} async-done(((f32[16,1,256]{2,1,0:T(1,128)}), f32[16,1,256]{2,1,0:T(1,128)S(1)}, u32[]{:S(2)}, u32[]{:S(2)}) %all-to-all-start.2) | async-done | bytes 16416 | tf_op jit(solution)/shard_map/all_to_all | solution.py:451
  143.6 0.6 copy.12
  144.2 1.3 lowest.1
  (44 shorter events, 0.2 us)
Async XLA Ops:
  0.6 16.1 %copy-start.3 = (bf16[256,768]{1,0:T(8,128)(2,1)S(1)}, bf16[256,768]{1,0:T(8,128)(2,1)}, u32[]{:S(2)}) copy-start(bf16[256,768]{1,0:T(8,128)(2,1)} %refs_3_.1) | copy-start | bytes 1179652
  1.7 2.8 %copy-start = (bf16[4096,768]{1,0:T(8,128)(2,1)S(1)}, bf16[4096,768]{1,0:T(8,128)(2,1)}, u32[]{:S(2)}) copy-start(bf16[4096,768]{1,0:T(8,128)(2,1)} %refs_1_.5) | copy-start | bytes 18874372
  4.5 74.3 %copy-start.4 = (bf16[768,128]{1,0:T(8,128)(2,1)S(1)}, bf16[768,128]{1,0:T(8,128)(2,1)}, u32[]{:S(2)}) copy-start(bf16[768,128]{1,0:T(8,128)(2,1)} %proj_ref.3) | copy-start | bytes 589828
  8.6 29.0 %all-to-all-start.1 = ((bf16[16,64,256]{2,1,0:T(8,128)(2,1)}), bf16[16,64,256]{2,1,0:T(8,128)(2,1)S(1)}, u32[]{:S(2)}, u32[]{:S(2)}) async-start(bf16[16,64,256]{2,1,0:T(8,128)(2,1)} %pack_prefixes.1), calls=%async_computation.1 | async-start | bytes 1048576 | tf_op jit(solution)/shard_map/all_to_all | solution.py:403
  16.8 12.8 %collective-permute-start = (bf16[256,256]{1,0:T(8,128)(2,1)S(1)}, bf16[256,256]{1,0:T(8,128)(2,1)S(1)}, u32[]{:S(2)}, u32[]{:S(2)}) collective-permute-start(bf16[256,256]{1,0:T(8,128)(2,1)S(1)} %slice.9), channel_id=1, source_target_pairs={{0,1},{1,2},{2,3},{3,0},{4,5},{5,6},{6,7},{7,4},{8,9},{9,10},{10,1... | collective-permute-start | bytes 393224 | tf_op jit(solution)/shard_map/ppermute | solution.py:390
  18.8 13.0 %collective-permute-start.1 = (bf16[256,256]{1,0:T(8,128)(2,1)S(1)}, bf16[256,256]{1,0:T(8,128)(2,1)S(1)}, u32[]{:S(2)}, u32[]{:S(2)}) collective-permute-start(bf16[256,256]{1,0:T(8,128)(2,1)S(1)} %slice.9), channel_id=1, source_target_pairs={{0,2},{1,3},{2,0},{3,1},{4,6},{5,7},{6,4},{7,5},{8,10},{9,11},{10,... | collective-permute-start | bytes 393224 | tf_op jit(solution)/shard_map/ppermute | solution.py:390
  21.5 10.4 %collective-permute-start.2 = (bf16[256,256]{1,0:T(8,128)(2,1)S(1)}, bf16[256,256]{1,0:T(8,128)(2,1)S(1)}, u32[]{:S(2)}, u32[]{:S(2)}) collective-permute-start(bf16[256,256]{1,0:T(8,128)(2,1)S(1)} %slice.9), channel_id=1, source_target_pairs={{0,3},{1,0},{2,1},{3,2},{4,7},{5,4},{6,5},{7,6},{8,11},{9,8},{10,9... | collective-permute-start | bytes 393224 | tf_op jit(solution)/shard_map/ppermute | solution.py:390
  32.7 40.8 %collective-permute-start.12 = (bf16[1024,256]{1,0:T(8,128)(2,1)}, bf16[1024,256]{1,0:T(8,128)(2,1)S(1)}, u32[]{:S(2)}, u32[]{:S(2)}) collective-permute-start(bf16[1024,256]{1,0:T(8,128)(2,1)} %pad_maximum_fusion), channel_id=1, source_target_pairs={{0,4},{1,5},{2,6},{3,7},{4,8},{5,9},{6,10},{7,11},{8,12},{9,13},{1... | collective-permute-start | bytes 1572872 | tf_op jit(solution)/shard_map/ppermute | solution.py:390
  34.1 41.0 %collective-permute-start.13 = (bf16[1024,256]{1,0:T(8,128)(2,1)}, bf16[1024,256]{1,0:T(8,128)(2,1)S(1)}, u32[]{:S(2)}, u32[]{:S(2)}) collective-permute-start(bf16[1024,256]{1,0:T(8,128)(2,1)} %pad_maximum_fusion), channel_id=1, source_target_pairs={{0,12},{1,13},{2,14},{3,15},{4,0},{5,1},{6,2},{7,3},{8,4},{9,5},{1... | collective-permute-start | bytes 1572872 | tf_op jit(solution)/shard_map/ppermute | solution.py:390
  35.9 40.8 %collective-permute-start.3 = (bf16[1024,256]{1,0:T(8,128)(2,1)}, bf16[1024,256]{1,0:T(8,128)(2,1)S(1)}, u32[]{:S(2)}, u32[]{:S(2)}) collective-permute-start(bf16[1024,256]{1,0:T(8,128)(2,1)} %pad_maximum_fusion), channel_id=1, source_target_pairs={{0,8},{1,9},{2,10},{3,11},{4,12},{5,13},{6,14},{7,15},{8,0},{9,1},... | collective-permute-start | bytes 1572872 | tf_op jit(solution)/shard_map/ppermute | solution.py:390
  38.8 39.1 %copy-start.15 = (f32[1,256]{1,0:T(1,128)}, f32[1,256]{1,0:T(1,128)S(1)}, u32[]{:S(2)}) copy-start(f32[1,256]{1,0:T(1,128)S(1)} %get-tuple-element.13.square_ref) | copy-start | bytes 3076
  38.8 6.2 %collective-permute-start.4 = (bf16[128,256]{1,0:T(8,128)(2,1)S(1)}, bf16[128,256]{1,0:T(8,128)(2,1)S(1)}, u32[]{:S(2)}, u32[]{:S(2)}) collective-permute-start(bf16[128,256]{1,0:T(8,128)(2,1)S(1)} %get-tuple-element.15.refs_4_), channel_id=1, source_target_pairs={{0,1},{1,2},{2,3},{3,0},{4,5},{5,6},{6,7},{7,4},{8,9},{9,10},{10,1... | collective-permute-start | bytes 196616 | tf_op jit(solution)/shard_map/ppermute | solution.py:390
  39.1 6.0 %collective-permute-start.5 = (bf16[128,256]{1,0:T(8,128)(2,1)S(1)}, bf16[128,256]{1,0:T(8,128)(2,1)S(1)}, u32[]{:S(2)}, u32[]{:S(2)}) collective-permute-start(bf16[128,256]{1,0:T(8,128)(2,1)S(1)} %get-tuple-element.15.refs_4_), channel_id=1, source_target_pairs={{0,2},{1,3},{2,0},{3,1},{4,6},{5,7},{6,4},{7,5},{8,10},{9,11},{10,... | collective-permute-start | bytes 196616 | tf_op jit(solution)/shard_map/ppermute | solution.py:390
  45.1 4.3 %collective-permute-start.6 = (bf16[128,256]{1,0:T(8,128)(2,1)S(1)}, bf16[128,256]{1,0:T(8,128)(2,1)S(1)}, u32[]{:S(2)}, u32[]{:S(2)}) collective-permute-start(bf16[128,256]{1,0:T(8,128)(2,1)S(1)} %get-tuple-element.15.refs_4_), channel_id=1, source_target_pairs={{0,3},{1,0},{2,1},{3,2},{4,7},{5,4},{6,5},{7,6},{8,11},{9,8},{10,9... | collective-permute-start | bytes 196616 | tf_op jit(solution)/shard_map/ppermute | solution.py:390
  45.1 14.6 %collective-permute-start.10 = (bf16[128,256]{1,0:T(8,128)(2,1)S(1)}, bf16[128,256]{1,0:T(8,128)(2,1)S(1)}, u32[]{:S(2)}, u32[]{:S(2)}) collective-permute-start(bf16[128,256]{1,0:T(8,128)(2,1)S(1)} %get-tuple-element.14.refs_5_), channel_id=1, source_target_pairs={{0,12},{1,13},{2,14},{3,15},{4,0},{5,1},{6,2},{7,3},{8,4},{9,5},{1... | collective-permute-start | bytes 196616 | tf_op jit(solution)/shard_map/ppermute | solution.py:390
  50.0 27.8 %collective-permute-start.14 = (bf16[512,256]{1,0:T(8,128)(2,1)}, bf16[512,256]{1,0:T(8,128)(2,1)S(1)}, u32[]{:S(2)}, u32[]{:S(2)}) collective-permute-start(bf16[512,256]{1,0:T(8,128)(2,1)} %pad_maximum_fusion.1), channel_id=1, source_target_pairs={{0,4},{1,5},{2,6},{3,7},{4,8},{5,9},{6,10},{7,11},{8,12},{9,13},{1... | collective-permute-start | bytes 786440 | tf_op jit(solution)/shard_map/ppermute | solution.py:390
  59.7 6.6 %collective-permute-start.8 = (bf16[128,256]{1,0:T(8,128)(2,1)S(1)}, bf16[128,256]{1,0:T(8,128)(2,1)S(1)}, u32[]{:S(2)}, u32[]{:S(2)}) collective-permute-start(bf16[128,256]{1,0:T(8,128)(2,1)S(1)} %get-tuple-element.14.refs_5_), channel_id=1, source_target_pairs={{0,4},{1,5},{2,6},{3,7},{4,8},{5,9},{6,10},{7,11},{8,12},{9,13},{1... | collective-permute-start | bytes 196616 | tf_op jit(solution)/shard_map/ppermute | solution.py:390
  66.3 5.8 %collective-permute-start.9 = (bf16[128,256]{1,0:T(8,128)(2,1)S(1)}, bf16[128,256]{1,0:T(8,128)(2,1)S(1)}, u32[]{:S(2)}, u32[]{:S(2)}) collective-permute-start(bf16[128,256]{1,0:T(8,128)(2,1)S(1)} %get-tuple-element.14.refs_5_), channel_id=1, source_target_pairs={{0,8},{1,9},{2,10},{3,11},{4,12},{5,13},{6,14},{7,15},{8,0},{9,1},... | collective-permute-start | bytes 196616 | tf_op jit(solution)/shard_map/ppermute | solution.py:390
  72.1 8.6 %copy-start.5 = (bf16[128,256]{1,0:T(8,128)(2,1)}, bf16[128,256]{1,0:T(8,128)(2,1)S(1)}, u32[]{:S(2)}) copy-start(bf16[128,256]{1,0:T(8,128)(2,1)S(1)} %collective-permute-done.9.refs_15_) | copy-start | bytes 196612
  72.1 35.2 %collective-permute-start.16 = (bf16[512,256]{1,0:T(8,128)(2,1)}, bf16[512,256]{1,0:T(8,128)(2,1)}, u32[]{:S(2)}, u32[]{:S(2)}) collective-permute-start(bf16[512,256]{1,0:T(8,128)(2,1)} %pad_maximum_fusion.1), channel_id=1, source_target_pairs={{0,12},{1,13},{2,14},{3,15},{4,0},{5,1},{6,2},{7,3},{8,4},{9,5},{1... | collective-permute-start | bytes 786440 | tf_op jit(solution)/shard_map/ppermute | solution.py:390
  73.4 33.9 %collective-permute-start.15 = (bf16[512,256]{1,0:T(8,128)(2,1)}, bf16[512,256]{1,0:T(8,128)(2,1)}, u32[]{:S(2)}, u32[]{:S(2)}) collective-permute-start(bf16[512,256]{1,0:T(8,128)(2,1)} %pad_maximum_fusion.2), channel_id=1, source_target_pairs={{0,1},{1,2},{2,3},{3,0},{4,5},{5,6},{6,7},{7,4},{8,9},{9,10},{10,1... | collective-permute-start | bytes 786440 | tf_op jit(solution)/shard_map/ppermute | solution.py:390
  75.1 32.2 %collective-permute-start.17 = (bf16[512,256]{1,0:T(8,128)(2,1)}, bf16[512,256]{1,0:T(8,128)(2,1)}, u32[]{:S(2)}, u32[]{:S(2)}) collective-permute-start(bf16[512,256]{1,0:T(8,128)(2,1)} %pad_maximum_fusion.2), channel_id=1, source_target_pairs={{0,3},{1,0},{2,1},{3,2},{4,7},{5,4},{6,5},{7,6},{8,11},{9,8},{10,9... | collective-permute-start | bytes 786440 | tf_op jit(solution)/shard_map/ppermute | solution.py:390
  76.7 44.5 %collective-permute-start.11 = (bf16[512,256]{1,0:T(8,128)(2,1)}, bf16[512,256]{1,0:T(8,128)(2,1)}, u32[]{:S(2)}, u32[]{:S(2)}) collective-permute-start(bf16[512,256]{1,0:T(8,128)(2,1)} %pad_maximum_fusion.2), channel_id=1, source_target_pairs={{0,2},{1,3},{2,0},{3,1},{4,6},{5,7},{6,4},{7,5},{8,10},{9,11},{10,... | collective-permute-start | bytes 786440 | tf_op jit(solution)/shard_map/ppermute | solution.py:390
  77.9 0.7 copy-start.7
  78.6 42.6 %collective-permute-start.7 = (bf16[512,256]{1,0:T(8,128)(2,1)}, bf16[512,256]{1,0:T(8,128)(2,1)}, u32[]{:S(2)}, u32[]{:S(2)}) collective-permute-start(bf16[512,256]{1,0:T(8,128)(2,1)} %pad_maximum_fusion.1), channel_id=1, source_target_pairs={{0,8},{1,9},{2,10},{3,11},{4,12},{5,13},{6,14},{7,15},{8,0},{9,1},... | collective-permute-start | bytes 786440 | tf_op jit(solution)/shard_map/ppermute | solution.py:390
  80.7 48.7 %all-to-all-start = ((bf16[128,8,128]{2,1,0:T(8,128)(2,1)}), bf16[128,8,128]{2,1,0:T(8,128)(2,1)S(1)}, u32[]{:S(2)}, u32[]{:S(2)}) async-start(bf16[128,8,128]{2,1,0:T(8,128)(2,1)} %outgoing_rows.1), calls=%async_computation | async-start | bytes 524288 | tf_op jit(solution)/shard_map/all_to_all | solution.py:415
  90.9 2.8 %copy-start.1 = (bf16[4096,768]{1,0:T(8,128)(2,1)S(1)}, bf16[4096,768]{1,0:T(8,128)(2,1)}, u32[]{:S(2)}) copy-start(bf16[4096,768]{1,0:T(8,128)(2,1)} %refs_1_.5) | copy-start | bytes 18874372
  93.7 6.3 %copy-start.2 = (bf16[4096,768]{1,0:T(8,128)(2,1)S(1)}, bf16[4096,768]{1,0:T(8,128)(2,1)}, u32[]{:S(2)}) copy-start(bf16[4096,768]{1,0:T(8,128)(2,1)} %refs_1_.5) | copy-start | bytes 18874372
  93.7 6.3 %copy-start.6 = (bf16[128,256]{1,0:T(8,128)(2,1)S(1)}, bf16[128,256]{1,0:T(8,128)(2,1)}, u32[]{:S(2)}) copy-start(bf16[128,256]{1,0:T(8,128)(2,1)} %copy-done.5) | copy-start | bytes 196612
  98.0 0.7 copy-start.9
  98.7 0.6 copy-start.11
  99.3 0.7 copy-start.13
  100.0 7.3 %copy-start.8 = (bf16[512,256]{1,0:T(8,128)(2,1)S(1)}, bf16[512,256]{1,0:T(8,128)(2,1)}, u32[]{:S(2)}) copy-start(bf16[512,256]{1,0:T(8,128)(2,1)} %copy-done.7) | copy-start | bytes 786436
  121.1 14.9 %copy-start.10 = (bf16[512,128]{1,0:T(8,128)(2,1)S(1)}, bf16[512,128]{1,0:T(8,128)(2,1)}, u32[]{:S(2)}) copy-start(bf16[512,128]{1,0:T(8,128)(2,1)} %copy-done.9) | copy-start | bytes 393220
  121.1 14.9 %copy-start.12 = (bf16[512,128]{1,0:T(8,128)(2,1)S(1)}, bf16[512,128]{1,0:T(8,128)(2,1)}, u32[]{:S(2)}) copy-start(bf16[512,128]{1,0:T(8,128)(2,1)} %copy-done.11) | copy-start | bytes 393220
  121.2 14.9 %copy-start.14 = (bf16[512,128]{1,0:T(8,128)(2,1)S(1)}, bf16[512,128]{1,0:T(8,128)(2,1)}, u32[]{:S(2)}) copy-start(bf16[512,128]{1,0:T(8,128)(2,1)} %copy-done.13) | copy-start | bytes 393220
  129.4 14.2 %all-to-all-start.2 = ((f32[16,1,256]{2,1,0:T(1,128)}), f32[16,1,256]{2,1,0:T(1,128)S(1)}, u32[]{:S(2)}, u32[]{:S(2)}) async-start(f32[16,1,256]{2,1,0:T(1,128)} %copy.6), calls=%async_computation.2 | async-start | bytes 32768 | tf_op jit(solution)/shard_map/all_to_all | solution.py:451

commit v2 on v0

v2 whole, which is shorter than its diff:
```python
import functools

import jax
import jax.numpy as jnp
from jax import lax
from jax.experimental import pallas as pl
from jax.experimental.pallas import tpu as pltpu
from jax.sharding import PartitionSpec as P

PREFIX = 256
N_DP = 8
N_LIST = 16
SIDE = 4
ROWS = 256
HALF = 128
LISTS = 4096
CAP = 8
SLOTS = N_DP * CAP
PDIM = 128

soar_weight = 1.5
masked_score = 1e30
NT = (((1,), (1,)), ((), ()))
bf16 = jnp.bfloat16
f32 = jnp.float32
i32 = jnp.int32


def iota(shape, dim):
    return lax.broadcasted_iota(i32, shape, dim)


def ones_where(mask):
    return jnp.where(mask, 1.0, 0.0)


def dot(a, b):
    return jnp.dot(a, b, preferred_element_type=f32)


def params(mib):
    return pltpu.CompilerParams(vmem_limit_bytes=mib << 20)


def split3(x):
    hi = x.astype(bf16)
    rest = x - hi.astype(f32)
    mid = rest.astype(bf16)
    low = (rest - mid.astype(f32)).astype(bf16)
    return hi, mid, low


def to_column(row, n):
    eye = iota((n, n), 0) == iota((n, n), 1)
    return jnp.sum(jnp.where(eye, jnp.broadcast_to(row, (n, n)), 0.0), axis=1, keepdims=True)


def to_row(column, n):
    eye = iota((n, n), 0) == iota((n, n), 1)
    return jnp.sum(jnp.where(eye, jnp.broadcast_to(column, (n, n)), 0.0), axis=0, keepdims=True)


VMEM = pl.BlockSpec(memory_space=pltpu.VMEM)
HBM = pl.BlockSpec(memory_space=pltpu.HBM)


def places():
    return lax.axis_index("dp"), lax.axis_index("list")


def call(kernel, name, mib, out_shape, *operands, hbm=(), scratch=()):
    return pl.pallas_call(
        kernel,
        out_shape=out_shape,
        in_specs=[HBM if n in hbm else VMEM for n in range(len(operands))],
        out_specs=jax.tree.map(lambda _: VMEM, out_shape),
        scratch_shapes=scratch,
        compiler_params=params(mib),
        name=name,
    )(*operands)


def pack_kernel(ids_ref, c_ref, out_ref):
    group, list_place = places()
    upto = ones_where(iota((ROWS, ROWS), 0) <= iota((ROWS, ROWS), 1)).astype(bf16)
    base = group * (N_LIST * ROWS)
    ids = jnp.concatenate(
        [
            ids_ref[0:1, pl.ds(pl.multiple_of(base + s * ROWS, ROWS), ROWS)]
            for s in range(N_LIST)
        ],
        axis=0,
    )
    inside = (ids >> 12) == list_place
    count = dot(ones_where(inside).astype(bf16), upto)
    rank = jnp.where(inside, count - 1.0, -1.0)
    local = (ids & (LISTS - 1)).astype(f32) + 1.0
    slot = iota((SLOTS, ROWS), 0).astype(f32)
    lane = iota((4 * SLOTS, LISTS), 1).astype(f32)
    for g in range(N_LIST // 4):
        picks = []
        for s in range(4 * g, 4 * g + 4):
            hit = slot == rank[s : s + 1, :]
            picks.append(jnp.sum(jnp.where(hit, local[s : s + 1, :], 0.0), axis=1, keepdims=True))
        pick = jnp.concatenate(picks, axis=0) - 1.0
        hot = ones_where(lane == pick).astype(bf16)
        out_ref[4 * g : 4 * g + 4] = (
            dot(hot, c_ref[...]).astype(bf16).reshape(4, SLOTS, PREFIX)
        )


def pack(ids, prefixes):
    shape = jax.ShapeDtypeStruct((N_LIST, SLOTS, PREFIX), bf16)
    return call(pack_kernel, "pack_prefixes", 16, shape, ids, prefixes)


def residual_kernel(
    ids_ref, got_ref, vec_hbm, keep_ref, send_ref, square_ref, head_ref, resid_ref, sem
):
    group, own = places()
    fetch = pltpu.make_async_copy(vec_hbm.at[:, pl.ds(0, PREFIX)], head_ref, sem)
    fetch.start()
    at = pl.multiple_of((group * N_LIST + own) * ROWS, ROWS)
    shard = ids_ref[0:1, pl.ds(at, ROWS)] >> 12
    member = iota((N_LIST, ROWS), 0) == shard
    upto = ones_where(iota((ROWS, ROWS), 0) <= iota((ROWS, ROWS), 1)).astype(bf16)
    count = dot(ones_where(member).astype(bf16), upto)
    rank = jnp.sum(jnp.where(member, count - 1.0, 0.0), axis=0, keepdims=True)
    slot = to_column((shard * SLOTS).astype(f32) + rank, ROWS)
    hot = ones_where(iota((ROWS, N_LIST * SLOTS), 1).astype(f32) == slot).astype(bf16)
    primary = dot(hot, got_ref[...].reshape(N_LIST * SLOTS, PREFIX))
    fetch.wait()
    head = head_ref[...].astype(f32)
    resid = (head - primary).astype(bf16).astype(f32)
    power = jnp.sum(resid * resid, axis=1, keepdims=True) * (1.0 / PREFIX) + 1e-6
    scale = jnp.sqrt(soar_weight / (PREFIX * power))
    resid_ref[...] = (resid * scale).astype(bf16)
    square_ref[...] = to_row(jnp.sum(head * head, axis=1, keepdims=True), ROWS)
    core = group % 2
    for half, to in ((core, keep_ref), (1 - core, send_ref)):
        rows = pl.ds(pl.multiple_of(half * HALF, HALF), HALF)
        to[:HALF] = head_ref[rows, :]
        to[HALF:] = resid_ref[rows, :]


def residuals(ids, got, vectors):
    halves = jax.ShapeDtypeStruct((2 * HALF, PREFIX), bf16)
    shape = (halves, halves, jax.ShapeDtypeStruct((1, ROWS), f32))
    scratch = [pltpu.VMEM((ROWS, PREFIX), bf16)] * 2 + [pltpu.SemaphoreType.DMA]
    return call(
        residual_kernel, "own_residuals", 8, shape, ids, got, vectors, hbm=(2,), scratch=scratch
    )


def rank_tables(first, second):
    before = ones_where(iota((ROWS, ROWS), 0) < iota((ROWS, ROWS), 1)).astype(bf16)
    one0, one1 = ones_where(first), ones_where(second)
    earlier = dot((one0 + one1).astype(bf16), before)
    return jnp.where(first, earlier, -1.0), jnp.where(second, earlier + one0, -1.0)


def eightfold(table):
    n = table.shape[0]
    return jnp.broadcast_to(table[:, None, :], (n, CAP, ROWS)).reshape(n * CAP, ROWS)


def prepare_kernel(
    ids_ref, c_hbm, vec_hbm, proj_ref, rows_ref, parts_ref, c_ref, vec_ref, sems
):
    group, own = places()
    step_rows = LISTS // 8
    wide = pltpu.make_async_copy(vec_hbm, vec_ref, sems.at[8])
    wide.start()
    copies = [
        pltpu.make_async_copy(
            c_hbm.at[pl.ds(n * step_rows, step_rows)],
            c_ref.at[pl.ds(n * step_rows, step_rows)],
            sems.at[n],
        )
        for n in range(8)
    ]
    for copy in copies:
        copy.start()
    at = pl.multiple_of((group * N_LIST + own) * ROWS, ROWS)
    devices = N_DP * N_LIST
    hits = []
    for k in range(2):
        ids = ids_ref[k : k + 1, pl.ds(at, ROWS)]
        hits.append(iota((devices, ROWS), 0) == (ids & (N_DP - 1)) * N_LIST + (ids >> 12))
    rank0, rank1 = rank_tables(*hits)
    slot = (iota((devices * CAP, ROWS), 0) & (CAP - 1)).astype(f32)
    hot = ones_where((eightfold(rank0) == slot) | (eightfold(rank1) == slot)).astype(bf16)
    wide.wait()
    payload = dot(vec_ref[...], proj_ref[...]).astype(bf16)
    rows_ref[...] = dot(hot, payload).astype(bf16).reshape(devices, CAP, PDIM)
    per = step_rows // N_DP
    chosen = iota((per, step_rows), 1) == N_DP * iota((per, step_rows), 0) + group
    chosen = ones_where(chosen).astype(bf16)
    for n, copy in enumerate(copies):
        copy.wait()
        mine = dot(chosen, c_ref[n * step_rows : (n + 1) * step_rows]).astype(bf16)
        for k, part in enumerate(split3(dot(mine, proj_ref[...]))):
            parts_ref[k, n * per : (n + 1) * per] = part


def prepare(ids, centroids, vectors, projection):
    shape = (
        jax.ShapeDtypeStruct((N_DP * N_LIST, CAP, PDIM), bf16),
        jax.ShapeDtypeStruct((3, LISTS // N_DP, PDIM), bf16),
    )
    scratch = [
        pltpu.VMEM(centroids.shape, bf16),
        pltpu.VMEM(vectors.shape, bf16),
        pltpu.SemaphoreType.DMA((9,)),
    ]
    return call(
        prepare_kernel, "prepare_rows", 56, shape, ids, centroids, vectors, projection, hbm=(1, 2), scratch=scratch
    )


def place_kernel(ids_ref, got_ref, parts_ref, out_ref):
    group, own = places()
    devices = N_DP * N_LIST
    hits, local = [], []
    for k in range(2):
        ids = ids_ref[k]
        hits.append(((ids & (N_DP - 1)) == group) & ((ids >> 12) == own))
        local.append(((ids & (LISTS - 1)) >> 3).astype(f32) + 1.0)
    rank0, rank1 = rank_tables(*hits)
    slot = (iota((devices * CAP, ROWS), 0) & (CAP - 1)).astype(f32)
    pick = jnp.where(eightfold(rank0) == slot, eightfold(local[0]), 0.0)
    pick += jnp.where(eightfold(rank1) == slot, eightfold(local[1]), 0.0)
    pick = jnp.sum(pick, axis=1, keepdims=True) - 1.0
    per_owner = LISTS // N_DP
    hot = ones_where(iota((devices * CAP, per_owner), 1).astype(f32) == pick).astype(bf16)
    centroid = dot(hot, parts_ref[0]) + dot(hot, parts_ref[1]) + dot(hot, parts_ref[2])
    got = got_ref[...].reshape(devices * CAP, PDIM).astype(f32)
    out_ref[...] = jnp.where(pick >= 0.0, got - centroid, 0.0).astype(bf16)


def placement(ids, got, parts):
    shape = jax.ShapeDtypeStruct((N_DP * N_LIST * CAP, PDIM), bf16)
    return call(place_kernel, "place_rows", 12, shape, ids, got, parts)


def squares_of(rows):
    square = jnp.square(rows.astype(f32))
    upper = square.astype(bf16)
    lower = (square - upper.astype(f32)).astype(bf16)
    one = jnp.ones((PREFIX, 128), bf16)
    return dot(upper, one) + dot(lower, one)


def score_kernel(steps, n_arrays, given, *refs):
    ids_ref, c_ref = refs[:2]
    arrays = refs[2 : 2 + n_arrays]
    rest = refs[2 + n_arrays :]
    if given == 2:
        square_ref, out_ref = rest[1:]
    else:
        out_ref, square_ref = rest[given:]
        square_ref[...] = squares_of(c_ref[...])
    out_ref[...] = rest[0][...] if given else jnp.zeros(out_ref.shape, f32)
    group, own = places()
    core = group % 2
    eye = iota((ROWS, ROWS), 0) == iota((ROWS, ROWS), 1)
    number = iota((LISTS, ROWS), 0)
    for n, (one, two) in enumerate(steps):
        dy = two + core * (one - two)
        dz = one + core * (two - one)
        spot = (own // SIDE + SIDE - dy) % SIDE * SIDE + (own % SIDE + SIDE - dz) % SIDE
        prims = []
        for k in range(2):
            device = (group + k * (1 - 2 * core)) * N_LIST + spot
            lane = pl.multiple_of(device * ROWS + core * HALF, HALF)
            prims.append(ids_ref[0:1, pl.ds(lane, HALF)] - own * LISTS)
        prim = jnp.concatenate(prims, axis=1)
        each = SIDE // n_arrays
        ref, at = arrays[n // each], n % each * 2 * ROWS
        parts = [ref[at + k * HALF : at + (k + 1) * HALF] for k in range(4)]
        head = jnp.concatenate([parts[0], parts[2]], axis=0)
        resid = jnp.concatenate([parts[1], parts[3]], axis=0)
        both = lax.dot_general(head, resid, NT, preferred_element_type=f32)
        cross = jnp.sum(jnp.where(eye, both, 0.0), axis=0, keepdims=True)
        dot_head = lax.dot_general(c_ref[...], head * bf16(-2), NT, preferred_element_type=f32)
        dot_resid = lax.dot_general(c_ref[...], resid, NT, preferred_element_type=f32)
        square = square_ref[...]
        square = jnp.concatenate([square, square], axis=1)
        along = cross - dot_resid
        score = (dot_head + square) + along * along
        score = jnp.where(number == prim, masked_score, score)
        low = jnp.min(score.reshape(LISTS // 8, 8, ROWS), axis=0)
        low = jnp.min(low, axis=0, keepdims=True)
        for k in range(2):
            out_ref[pl.ds(spot, 1), k : k + 1, :] = low[:, k * HALF : (k + 1) * HALF][None]


def scores(name, ids, prefixes, arrays, steps, *last):
    out = jax.ShapeDtypeStruct((N_LIST, 8, HALF), f32)
    return call(
        functools.partial(score_kernel, steps, len(arrays), len(last)),
        name,
        28,
        out if len(last) == 2 else (out, jax.ShapeDtypeStruct((LISTS, 128), f32)),
        ids,
        prefixes,
        *arrays,
        *last,
    )


STEPS = (1, 3, 2)


def move(x, distance, second):
    pairs = []
    for dp in range(N_DP):
        for at in range(N_LIST):
            y, z = divmod(at, SIDE)
            if (dp % 2 == 1) != second:
                y = (y + distance) % SIDE
            else:
                z = (z + distance) % SIDE
            pairs.append((dp * N_LIST + at, dp * N_LIST + y * SIDE + z))
    return lax.ppermute(x, ("dp", "list"), pairs)


def from_other_core(x):
    return lax.ppermute(x, "dp", [(at, at ^ 1) for at in range(N_DP)])


def together(*xs):
    return lax.optimization_barrier(xs)


def local(vectors, centroids, projection, list_ids):
    ids = list_ids.T
    id_rows = ids.reshape(2, N_DP * N_LIST, ROWS)

    prefixes = centroids[:, :PREFIX]
    slots, projection = together(pack(ids, prefixes), projection)
    got = lax.all_to_all(slots, "list", 0, 0, tiled=True)
    rows_out, parts = prepare(ids, centroids, vectors, projection)
    got, rows_out = together(got, rows_out)
    keep, send, head_square = residuals(ids, got, vectors)

    block = jnp.concatenate([keep, from_other_core(send)], axis=0)
    block, rows_out = together(block, rows_out)
    blocks = [block] + [move(block, d, False) for d in STEPS]
    rows_in = lax.all_to_all(rows_out, ("dp", "list"), 0, 0, tiled=True)
    pairs = [jnp.concatenate(blocks[k : k + 2], axis=0) for k in (0, 2)]
    ahead, behind, ahead_too, behind_too = (
        move(pairs[k], STEPS[n], True) for k, n in ((0, 0), (1, 1), (1, 0), (0, 1))
    )
    steps = [[(a, d) for a in (0,) + STEPS] for d in (0,) + STEPS]
    lowest, _ = scores("scores_near", ids, prefixes, blocks, steps[0])
    _, to_far, from_far, rows_in = together(lowest, ahead, behind, rows_in)
    far = [move(to_far, STEPS[0], True), move(from_far, STEPS[1], True)]
    lowest, square = scores("scores_right", ids, prefixes, [ahead, ahead_too], steps[1], lowest)
    lowest = scores("scores_left", ids, prefixes, [behind_too, behind], steps[2], lowest, square)
    lowest = scores("scores_far", ids, prefixes, far, steps[3], lowest, square)
    back = lax.all_to_all(lowest, "list", 0, 0, tiled=True)
    placed = placement(id_rows, rows_in, parts)
    back, placed = together(back, placed)
    low = jnp.min(back[:, :2], axis=0)
    other = from_other_core(low[1:])
    core = lax.axis_index("dp") % 2
    low = jnp.where(iota((2, HALF), 0) == core, low[:1], other)
    lowest_score = (low.reshape(ROWS) + head_square.reshape(ROWS)) / PREFIX
    return placed, lowest_score


def solution(mesh):
    return jax.shard_map(
        local,
        mesh=mesh,
        in_specs=(P(("dp", "list"), None), P("list", None), P(), P()),
        out_specs=(P(("dp", "list"), None), P(("dp", "list"))),
        check_vma=False,
    )
```

time: 406 us -> 97.9 us (0.24)
  waiting for transfers between devices: 110 us -> 18.8 us
  other arithmetic: 75.1 us -> 0.68 us
  blocking collectives: 72.2 us -> 0 us
  matrix products: 62.9 us -> 0 us
  local copies, waits for them, and re-layouts: 63 us -> 5.73 us
  Pallas kernels: 0 us -> 39.5 us
  starting transfers between devices: 8.09 us -> 30.8 us
  between operations: 14.1 us -> 0.83 us
    pmin x1 -> x0, blocking collectives: 72.2 us -> none  [local(): group_lowest = lax.pmin(partial_value, 'list')]
    reduce_scatter x1 -> x0, waiting for transfers between devices: 66.4 us -> none  [local(): lax.psum_scatter(jnp.where(inside[:, None], picked.astype(jnp.float32), 0...]
    dot_general x6 -> x0, matrix products: 62.9 us -> none  [the longest x4 61.2 us: sweep_block(): lax.dot_general(stacked, block, (((1,), (1,)), ((), ())), preferred_eleme...]
    reduce_min x4 -> x1, other arithmetic: 51.7 us -> 0.03 us  [local(): low = jnp.min(back[:, :2], axis=0)]
    all_gather x2 -> x0, waiting for transfers between devices: 43.5 us -> none  [local(): lax.all_gather((head_prefix, residual), 'list', axis=0, tiled=True)]
    pallas_call x0 -> x8, Pallas kernels: none -> 39.5 us  [call(): pl.pallas_call(kernel, out_shape=out_shape, in_specs=[HBM if n in hbm els...]
    reshape x5 -> x0, local copies, waits for them, and re-layouts: 25.8 us -> none  [the longest x3 25.5 us: local(): all_ids = list_ids.reshape(device_count, -1)]
    gather x2 -> x0, local copies, waits for them, and re-layouts: 19.7 us -> none  [the longest x1 16.9 us: local(): jnp.take(centroid_prefix, jnp.clip(local_index, 0, per_device - 1), axis=0)]
  transfers between devices with their start and end apart: 4 -> 14, of which waited for: 2 -> 7; matrix products, arithmetic and copies ran while one was open for 14% -> 3% of each run, Pallas kernels for 0% -> 31%
where the time goes in v2:
time: 97.9 us; the launch traced here: 96.4 us
  Pallas kernels  39.5 us (40%)
  starting transfers between devices  30.8 us (31%)
  waiting for transfers between devices  18.8 us (19%)
  local copies, waits for them, and re-layouts  5.73 us (6%)
    pallas_call x8, Pallas kernels, call(): pl.pallas_call(kernel, out_shape=out_shape, in_specs=[HBM if n in hbm els...  39.5 us
    ppermute x9, starting transfers between devices, move(): return lax.ppermute(x, ('dp', 'list'), pairs)  12 us
    all_to_all x1, starting transfers between devices, local(): got = lax.all_to_all(slots, 'list', 0, 0, tiled=True)  8.13 us
    ppermute x9, waiting for transfers between devices, move(): return lax.ppermute(x, ('dp', 'list'), pairs)  6.57 us
    all_to_all x1, starting transfers between devices, local(): rows_in = lax.all_to_all(rows_out, ('dp', 'list'), 0, 0, tiled=True)  6.16 us
    all_to_all x1, waiting for transfers between devices, local(): back = lax.all_to_all(lowest, 'list', 0, 0, tiled=True)  5.28 us
    all_to_all x1, waiting for transfers between devices, local(): got = lax.all_to_all(slots, 'list', 0, 0, tiled=True)  4.48 us
    all_to_all x1, starting transfers between devices, local(): back = lax.all_to_all(lowest, 'list', 0, 0, tiled=True)  4.36 us
  transfers between devices with their start and end apart: 14, of which 7 were waited for; matrix products, arithmetic and copies ran while one was open for 3% of the time, Pallas kernels for 31%

profile of v2, /device:TPU:0, one launch (start us, length us, event | category | flops | bytes accessed | tf_op | source)
XLA Modules:
  0.0 96.4 jit_solution(13252264511332145607)
XLA Ops:
  0.6 0.0 copy-start
  0.6 1.8 %slice.12.c_ref.refs_1_ = bf16[4096,256]{1,0:T(8,128)(2,1)S(1)} slice(bf16[4096,768]{1,0:T(8,128)(2,1)} %c_hbm.1), slice={[0:4096], [0:256]} | slice | bytes 4194304 | tf_op jit(solution)/shard_map/slice | solution.py:340
  2.4 3.5 %pack_prefixes.1 = bf16[16,64,256]{2,1,0:T(8,128)(2,1)} custom-call(s32[2,32768]{1,0:T(2,128)S(1)} %bitcast.14, bf16[4096,256]{1,0:T(8,128)(2,1)S(1)} %slice.12.c_ref.refs_1_), custom_call_target="tpu_custom_call" | custom-call | tf_op jit(solution)/shard_map/pack_prefixes/pallas_call | solution.py:72
  6.0 8.1 %all-to-all-start = ((bf16[16,64,256]{2,1,0:T(8,128)(2,1)}), bf16[16,64,256]{2,1,0:T(8,128)(2,1)S(1)}, u32[]{:S(2)}, u32[]{:S(2)}) async-start(bf16[16,64,256]{2,1,0:T(8,128)(2,1)} %pack_prefixes.1), calls=%async_computation | async-start | bytes 1048576 | tf_op jit(solution)/shard_map/all_to_all | solution.py:342
  14.1 0.0 copy-start.1
  14.1 0.0 copy-start.2
  14.1 7.0 %prepare_rows.1 = (bf16[128,8,128]{2,1,0:T(8,128)(2,1)}, bf16[3,512,128]{2,1,0:T(8,128)(2,1)}) custom-call(s32[2,32768]{1,0:T(2,128)} %bitcast.13, bf16[4096,768]{1,0:T(8,128)(2,1)} %c_hbm.1, bf16[256,768]{1,0:T(8,128)(2,1)} %vec_hbm.3, bf16[768,128]{1,0:T(8,128)(2,1)} %proj_ref), custom_call_target="tpu_custom_call" | custom-call | tf_op jit(solution)/shard_map/prepare_rows/pallas_call | solution.py:72
  21.1 4.5 %all-to-all-done.got_ref = bf16[16,64,256]{2,1,0:T(8,128)(2,1)S(1)} async-done(((bf16[16,64,256]{2,1,0:T(8,128)(2,1)}), bf16[16,64,256]{2,1,0:T(8,128)(2,1)S(1)}, u32[]{:S(2)}, u32[]{:S(2)}) %all-to-all-start) | async-done | bytes 524320 | tf_op jit(solution)/shard_map/all_to_all | solution.py:342
  25.6 0.0 copy-done.2
  25.6 0.8 own_residuals.1
  26.4 0.1 collective-permute-start
  26.5 1.3 %collective-permute-done = bf16[256,256]{1,0:T(8,128)(2,1)S(1)} collective-permute-done((bf16[256,256]{1,0:T(8,128)(2,1)S(1)}, bf16[256,256]{1,0:T(8,128)(2,1)S(1)}, u32[]{:S(2)}, u32[]{:S(2)}) %collective-permute-start) | collective-permute-done | bytes 131104 | tf_op jit(solution)/shard_map/ppermute | solution.py:329
  27.8 0.6 collective-permute-start.1
  28.4 2.7 %collective-permute-start.2 = (bf16[512,256]{1,0:T(8,128)(2,1)S(1)}, bf16[512,256]{1,0:T(8,128)(2,1)S(1)}, u32[]{:S(2)}, u32[]{:S(2)}) collective-permute-start(bf16[512,256]{1,0:T(8,128)(2,1)S(1)} %pad_maximum_fusion.refs_2_), channel_id=1, source_target_pairs={{0,3},{1,0},{2,1},{3,2},{4,7},{5,4},{6,5},{7,6},{8,11},{9,8},{10,9... | collective-permute-start | bytes 786440 | tf_op jit(solution)/shard_map/ppermute | solution.py:325
  31.1 0.0 collective-permute-start.3
  31.1 0.7 constant_dynamic-update-slice_fusion.1
  31.8 3.6 %collective-permute-done.1.refs_3_ = bf16[512,256]{1,0:T(8,128)(2,1)S(1)} collective-permute-done((bf16[512,256]{1,0:T(8,128)(2,1)S(1)}, bf16[512,256]{1,0:T(8,128)(2,1)S(1)}, u32[]{:S(2)}, u32[]{:S(2)}) %collective-permute-start.1) | collective-permute-done | bytes 262176 | tf_op jit(solution)/shard_map/ppermute | solution.py:325
  35.5 0.7 constant_dynamic-update-slice_fusion
  36.2 0.0 collective-permute-start.4
  36.2 1.6 %collective-permute-done.2.refs_4_ = bf16[512,256]{1,0:T(8,128)(2,1)S(1)} collective-permute-done((bf16[512,256]{1,0:T(8,128)(2,1)S(1)}, bf16[512,256]{1,0:T(8,128)(2,1)S(1)}, u32[]{:S(2)}, u32[]{:S(2)}) %collective-permute-start.2) | collective-permute-done | bytes 262176 | tf_op jit(solution)/shard_map/ppermute | solution.py:325
  37.8 0.7 constant_dynamic-update-slice_fusion.3
  38.6 1.3 %collective-permute-done.3.refs_5_ = bf16[512,256]{1,0:T(8,128)(2,1)S(1)} collective-permute-done((bf16[512,256]{1,0:T(8,128)(2,1)S(1)}, bf16[512,256]{1,0:T(8,128)(2,1)S(1)}, u32[]{:S(2)}, u32[]{:S(2)}) %collective-permute-start.3) | collective-permute-done | bytes 262176 | tf_op jit(solution)/shard_map/ppermute | solution.py:325
  39.9 0.8 constant_dynamic-update-slice_fusion.2
  40.6 2.1 %collective-permute-start.5 = (bf16[1024,256]{1,0:T(8,128)(2,1)}, bf16[1024,256]{1,0:T(8,128)(2,1)}, u32[]{:S(2)}, u32[]{:S(2)}) collective-permute-start(bf16[1024,256]{1,0:T(8,128)(2,1)} %constant_dynamic-update-slice_fusion.2), channel_id=1, source_target_pairs={{0,12},{1,13},{2,14},{3,15},{4,0},{5,1},{6,2},{7,3},{8,4},{9,5},{1... | collective-permute-start | bytes 1572872 | tf_op jit(solution)/shard_map/ppermute | solution.py:325
  42.7 0.0 copy-done.3
  42.7 6.2 %all-to-all-start.1 = ((bf16[128,8,128]{2,1,0:T(8,128)(2,1)}), bf16[128,8,128]{2,1,0:T(8,128)(2,1)S(1)}, u32[]{:S(2)}, u32[]{:S(2)}) async-start(bf16[128,8,128]{2,1,0:T(8,128)(2,1)} %get-tuple-element.30), calls=%async_computation.1 | async-start | bytes 524288 | tf_op jit(solution)/shard_map/all_to_all | solution.py:350
  48.9 1.0 %collective-permute-start.9 = (bf16[1024,256]{1,0:T(8,128)(2,1)}, bf16[1024,256]{1,0:T(8,128)(2,1)}, u32[]{:S(2)}, u32[]{:S(2)}) collective-permute-start(bf16[1024,256]{1,0:T(8,128)(2,1)} %constant_dynamic-update-slice_fusion.2), channel_id=1, source_target_pairs={{0,4},{1,5},{2,6},{3,7},{4,8},{5,9},{6,10},{7,11},{8,12},{9,13},{1... | collective-permute-start | bytes 1572872 | tf_op jit(solution)/shard_map/ppermute | solution.py:325
  49.9 2.3 %collective-permute-start.8 = (bf16[1024,256]{1,0:T(8,128)(2,1)}, bf16[1024,256]{1,0:T(8,128)(2,1)}, u32[]{:S(2)}, u32[]{:S(2)}) collective-permute-start(bf16[1024,256]{1,0:T(8,128)(2,1)} %constant_dynamic-update-slice_fusion), channel_id=1, source_target_pairs={{0,12},{1,13},{2,14},{3,15},{4,0},{5,1},{6,2},{7,3},{8,4},{9,5},{1... | collective-permute-start | bytes 1572872 | tf_op jit(solution)/shard_map/ppermute | solution.py:325
  52.2 0.9 copy-done.4
  53.1 7.1 %scores_near.1 = (f32[16,8,128]{2,1,0:T(8,128)S(1)}, f32[4096,128]{1,0:T(8,128)}) custom-call(s32[2,32768]{1,0:T(2,128)S(1)} %bitcast.16, bf16[4096,256]{1,0:T(8,128)(2,1)S(1)} %slice.12.c_ref.refs_1_, bf16[512,256]{1,0:T(8,128)(2,1)S(1)} %pad_maximum_fusion.refs_2_, bf16[512,256]{1,0:T(8,128)(2,1)S(1)} %collective-permute-done.1.refs_3_, ...), custom_call_target="tpu_custom_call" | custom-call | tf_op jit(solution)/shard_map/scores_near/pallas_call | solution.py:72
  60.3 0.0 all-to-all-done.1.got_ref
  60.3 0.0 collective-permute-done.4.refs_2_
  60.3 0.0 collective-permute-done.5.refs_3_
  60.3 0.2 collective-permute-start.6
  60.5 3.1 %collective-permute-start.7 = (bf16[1024,256]{1,0:T(8,128)(2,1)}, bf16[1024,256]{1,0:T(8,128)(2,1)S(1)}, u32[]{:S(2)}, u32[]{:S(2)}) collective-permute-start(bf16[1024,256]{1,0:T(8,128)(2,1)} %collective-permute-done.5.refs_3_), channel_id=1, source_target_pairs={{0,12},{1,13},{2,14},{3,15},{4,0},{5,1},{6,2},{7,3},{8,4},{9,5},{1... | collective-permute-start | bytes 1572872 | tf_op jit(solution)/shard_map/ppermute | solution.py:325
  63.6 0.0 collective-permute-done.9.refs_3_
  63.6 7.1 %scores_right.1 = (f32[16,8,128]{2,1,0:T(8,128)S(1)}, f32[4096,128]{1,0:T(8,128)S(1)}) custom-call(s32[2,32768]{1,0:T(2,128)S(1)} %bitcast.17, bf16[4096,256]{1,0:T(8,128)(2,1)S(1)} %slice.12.c_ref.refs_1_, bf16[1024,256]{1,0:T(8,128)(2,1)} %collective-permute-done.4.refs_2_, bf16[1024,256]{1,0:T(8,128)(2,1)} %collective-permute-done.9.refs_3_, ...), custom_call_target="tpu_custom_call" | custom-call | tf_op jit(solution)/shard_map/scores_right/pallas_call | solution.py:72
  70.7 0.0 collective-permute-done.8.refs_2_
  70.7 6.0 %scores_left.1.refs_4_ = f32[16,8,128]{2,1,0:T(8,128)S(1)} custom-call(s32[2,32768]{1,0:T(2,128)S(1)} %bitcast.18, bf16[4096,256]{1,0:T(8,128)(2,1)S(1)} %slice.12.c_ref.refs_1_, bf16[1024,256]{1,0:T(8,128)(2,1)} %collective-permute-done.8.refs_2_, bf16[1024,256]{1,0:T(8,128)(2,1)} %collective-permute-done.5.refs_3_, ...), custom_call_target="tpu_custom_call" | custom-call | tf_op jit(solution)/shard_map/scores_left/pallas_call | solution.py:72
  76.8 0.0 collective-permute-done.6.refs_2_
  76.8 0.0 collective-permute-done.7.refs_3_
  76.8 5.7 %scores_far.1 = f32[16,8,128]{2,1,0:T(8,128)} custom-call(s32[2,32768]{1,0:T(2,128)S(1)} %bitcast.19, bf16[4096,256]{1,0:T(8,128)(2,1)S(1)} %slice.12.c_ref.refs_1_, bf16[1024,256]{1,0:T(8,128)(2,1)S(1)} %collective-permute-done.6.refs_2_, bf16[1024,256]{1,0:T(8,128)(2,1)S(1)} %collective-permute-done.7.refs_3_, f32[16,8,128]{2,1,0:T(8,128)S(1)} %scores_left.1.refs_4_, ...), custom_call_target="tpu_custom_call" | custom-call | tf_op jit(solution)/shard_map/scores_far/pallas_call | solution.py:72
  82.5 4.4 %all-to-all-start.2 = ((f32[16,8,128]{2,1,0:T(8,128)}), f32[16,8,128]{2,1,0:T(8,128)S(1)}, u32[]{:S(2)}, u32[]{:S(2)}) async-start(f32[16,8,128]{2,1,0:T(8,128)} %scores_far.1), calls=%async_computation.2 | async-start | bytes 131072 | tf_op jit(solution)/shard_map/all_to_all | solution.py:362
  86.9 2.3 %place_rows.1 = bf16[1024,128]{1,0:T(8,128)(2,1)} custom-call(s32[2,128,256]{2,1,0:T(8,128)S(1)} %bitcast.21, bf16[128,8,128]{2,1,0:T(8,128)(2,1)S(1)} %all-to-all-done.1.got_ref, bf16[3,512,128]{2,1,0:T(8,128)(2,1)S(1)} %copy-done.5), custom_call_target="tpu_custom_call" | custom-call | tf_op jit(solution)/shard_map/place_rows/pallas_call | solution.py:72
  89.2 5.3 %all-to-all-done.2 = f32[16,8,128]{2,1,0:T(8,128)S(1)} async-done(((f32[16,8,128]{2,1,0:T(8,128)}), f32[16,8,128]{2,1,0:T(8,128)S(1)}, u32[]{:S(2)}, u32[]{:S(2)}) %all-to-all-start.2) | async-done | bytes 65568 | tf_op jit(solution)/shard_map/all_to_all | solution.py:362
  94.5 0.1 collective-permute-start.10
  94.6 1.1 %collective-permute-done.10 = f32[1,128]{1,0:T(1,128)S(1)} collective-permute-done((f32[1,128]{1,0:T(1,128)S(1)}, f32[1,128]{1,0:T(1,128)S(1)}, u32[]{:S(2)}, u32[]{:S(2)}) %collective-permute-start.10) | collective-permute-done | bytes 544 | tf_op jit(solution)/shard_map/ppermute | solution.py:329
  95.7 0.6 fusion
  (11 shorter events, 0.1 us)
Async XLA Ops:
  0.6 1.8 %copy-start = (s32[32768,2]{0,1:T(2,128)S(1)}, s32[32768,2]{0,1:T(2,128)}, u32[]{:S(2)}) copy-start(s32[32768,2]{0,1:T(2,128)} %param.7) | copy-start | bytes 786436
  6.0 19.6 %all-to-all-start = ((bf16[16,64,256]{2,1,0:T(8,128)(2,1)}), bf16[16,64,256]{2,1,0:T(8,128)(2,1)S(1)}, u32[]{:S(2)}, u32[]{:S(2)}) async-start(bf16[16,64,256]{2,1,0:T(8,128)(2,1)} %pack_prefixes.1), calls=%async_computation | async-start | bytes 1048576 | tf_op jit(solution)/shard_map/all_to_all | solution.py:342
  14.1 11.5 %copy-start.1 = (s32[32768,2]{0,1:T(2,128)S(1)}, s32[32768,2]{0,1:T(2,128)}, u32[]{:S(2)}) copy-start(s32[32768,2]{0,1:T(2,128)} %param.7) | copy-start | bytes 786436
  14.1 11.5 %copy-start.2 = (bf16[256,768]{1,0:T(8,128)(2,1)S(1)}, bf16[256,768]{1,0:T(8,128)(2,1)}, u32[]{:S(2)}) copy-start(bf16[256,768]{1,0:T(8,128)(2,1)} %vec_hbm.3) | copy-start | bytes 1179652
  26.4 1.4 %collective-permute-start = (bf16[256,256]{1,0:T(8,128)(2,1)S(1)}, bf16[256,256]{1,0:T(8,128)(2,1)S(1)}, u32[]{:S(2)}, u32[]{:S(2)}) collective-permute-start(bf16[256,256]{1,0:T(8,128)(2,1)S(1)} %get-tuple-element.26), channel_id=1, source_target_pairs={{0,16},{16,0},{32,48},{48,32},{64,80},{80,64},{96,112},{112,96},{1... | collective-permute-start | bytes 393224 | tf_op jit(solution)/shard_map/ppermute | solution.py:329
  27.8 7.7 %collective-permute-start.1 = (bf16[512,256]{1,0:T(8,128)(2,1)S(1)}, bf16[512,256]{1,0:T(8,128)(2,1)S(1)}, u32[]{:S(2)}, u32[]{:S(2)}) collective-permute-start(bf16[512,256]{1,0:T(8,128)(2,1)S(1)} %pad_maximum_fusion.refs_2_), channel_id=1, source_target_pairs={{0,1},{1,2},{2,3},{3,0},{4,5},{5,6},{6,7},{7,4},{8,9},{9,10},{10,1... | collective-permute-start | bytes 786440 | tf_op jit(solution)/shard_map/ppermute | solution.py:325
  28.4 9.4 %collective-permute-start.2 = (bf16[512,256]{1,0:T(8,128)(2,1)S(1)}, bf16[512,256]{1,0:T(8,128)(2,1)S(1)}, u32[]{:S(2)}, u32[]{:S(2)}) collective-permute-start(bf16[512,256]{1,0:T(8,128)(2,1)S(1)} %pad_maximum_fusion.refs_2_), channel_id=1, source_target_pairs={{0,3},{1,0},{2,1},{3,2},{4,7},{5,4},{6,5},{7,6},{8,11},{9,8},{10,9... | collective-permute-start | bytes 786440 | tf_op jit(solution)/shard_map/ppermute | solution.py:325
  31.1 8.7 %collective-permute-start.3 = (bf16[512,256]{1,0:T(8,128)(2,1)S(1)}, bf16[512,256]{1,0:T(8,128)(2,1)S(1)}, u32[]{:S(2)}, u32[]{:S(2)}) collective-permute-start(bf16[512,256]{1,0:T(8,128)(2,1)S(1)} %pad_maximum_fusion.refs_2_), channel_id=1, source_target_pairs={{0,2},{1,3},{2,0},{3,1},{4,6},{5,7},{6,4},{7,5},{8,10},{9,11},{10,... | collective-permute-start | bytes 786440 | tf_op jit(solution)/shard_map/ppermute | solution.py:325
  36.2 24.1 %collective-permute-start.4 = (bf16[1024,256]{1,0:T(8,128)(2,1)}, bf16[1024,256]{1,0:T(8,128)(2,1)}, u32[]{:S(2)}, u32[]{:S(2)}) collective-permute-start(bf16[1024,256]{1,0:T(8,128)(2,1)} %constant_dynamic-update-slice_fusion), channel_id=1, source_target_pairs={{0,4},{1,5},{2,6},{3,7},{4,8},{5,9},{6,10},{7,11},{8,12},{9,13},{1... | collective-permute-start | bytes 1572872 | tf_op jit(solution)/shard_map/ppermute | solution.py:325
  39.9 2.9 %copy-start.3 = (bf16[512,256]{1,0:T(8,128)(2,1)}, bf16[512,256]{1,0:T(8,128)(2,1)S(1)}, u32[]{:S(2)}) copy-start(bf16[512,256]{1,0:T(8,128)(2,1)S(1)} %collective-permute-done.3.refs_5_) | copy-start | bytes 786436
  40.6 19.7 %collective-permute-start.5 = (bf16[1024,256]{1,0:T(8,128)(2,1)}, bf16[1024,256]{1,0:T(8,128)(2,1)}, u32[]{:S(2)}, u32[]{:S(2)}) collective-permute-start(bf16[1024,256]{1,0:T(8,128)(2,1)} %constant_dynamic-update-slice_fusion.2), channel_id=1, source_target_pairs={{0,12},{1,13},{2,14},{3,15},{4,0},{5,1},{6,2},{7,3},{8,4},{9,5},{1... | collective-permute-start | bytes 1572872 | tf_op jit(solution)/shard_map/ppermute | solution.py:325
  42.7 17.6 %all-to-all-start.1 = ((bf16[128,8,128]{2,1,0:T(8,128)(2,1)}), bf16[128,8,128]{2,1,0:T(8,128)(2,1)S(1)}, u32[]{:S(2)}, u32[]{:S(2)}) async-start(bf16[128,8,128]{2,1,0:T(8,128)(2,1)} %get-tuple-element.30), calls=%async_computation.1 | async-start | bytes 524288 | tf_op jit(solution)/shard_map/all_to_all | solution.py:350
  48.9 14.7 %collective-permute-start.9 = (bf16[1024,256]{1,0:T(8,128)(2,1)}, bf16[1024,256]{1,0:T(8,128)(2,1)}, u32[]{:S(2)}, u32[]{:S(2)}) collective-permute-start(bf16[1024,256]{1,0:T(8,128)(2,1)} %constant_dynamic-update-slice_fusion.2), channel_id=1, source_target_pairs={{0,4},{1,5},{2,6},{3,7},{4,8},{5,9},{6,10},{7,11},{8,12},{9,13},{1... | collective-permute-start | bytes 1572872 | tf_op jit(solution)/shard_map/ppermute | solution.py:325
  49.9 20.8 %collective-permute-start.8 = (bf16[1024,256]{1,0:T(8,128)(2,1)}, bf16[1024,256]{1,0:T(8,128)(2,1)}, u32[]{:S(2)}, u32[]{:S(2)}) collective-permute-start(bf16[1024,256]{1,0:T(8,128)(2,1)} %constant_dynamic-update-slice_fusion), channel_id=1, source_target_pairs={{0,12},{1,13},{2,14},{3,15},{4,0},{5,1},{6,2},{7,3},{8,4},{9,5},{1... | collective-permute-start | bytes 1572872 | tf_op jit(solution)/shard_map/ppermute | solution.py:325
  52.2 0.9 copy-start.4
  60.3 16.5 %collective-permute-start.6 = (bf16[1024,256]{1,0:T(8,128)(2,1)}, bf16[1024,256]{1,0:T(8,128)(2,1)S(1)}, u32[]{:S(2)}, u32[]{:S(2)}) collective-permute-start(bf16[1024,256]{1,0:T(8,128)(2,1)} %collective-permute-done.4.refs_2_), channel_id=1, source_target_pairs={{0,4},{1,5},{2,6},{3,7},{4,8},{5,9},{6,10},{7,11},{8,12},{9,13},{1... | collective-permute-start | bytes 1572872 | tf_op jit(solution)/shard_map/ppermute | solution.py:325
  60.5 16.2 %collective-permute-start.7 = (bf16[1024,256]{1,0:T(8,128)(2,1)}, bf16[1024,256]{1,0:T(8,128)(2,1)S(1)}, u32[]{:S(2)}, u32[]{:S(2)}) collective-permute-start(bf16[1024,256]{1,0:T(8,128)(2,1)} %collective-permute-done.5.refs_3_), channel_id=1, source_target_pairs={{0,12},{1,13},{2,14},{3,15},{4,0},{5,1},{6,2},{7,3},{8,4},{9,5},{1... | collective-permute-start | bytes 1572872 | tf_op jit(solution)/shard_map/ppermute | solution.py:325
  76.7 10.1 %copy-start.5 = (bf16[3,512,128]{2,1,0:T(8,128)(2,1)S(1)}, bf16[3,512,128]{2,1,0:T(8,128)(2,1)}, u32[]{:S(2)}) copy-start(bf16[3,512,128]{2,1,0:T(8,128)(2,1)} %get-tuple-element.36.parts_ref) | copy-start | bytes 1179652
  82.5 12.0 %all-to-all-start.2 = ((f32[16,8,128]{2,1,0:T(8,128)}), f32[16,8,128]{2,1,0:T(8,128)S(1)}, u32[]{:S(2)}, u32[]{:S(2)}) async-start(f32[16,8,128]{2,1,0:T(8,128)} %scores_far.1), calls=%async_computation.2 | async-start | bytes 131072 | tf_op jit(solution)/shard_map/all_to_all | solution.py:362
  94.5 1.2 %collective-permute-start.10 = (f32[1,128]{1,0:T(1,128)S(1)}, f32[1,128]{1,0:T(1,128)S(1)}, u32[]{:S(2)}, u32[]{:S(2)}) collective-permute-start(f32[1,128]{1,0:T(1,128)S(1)} %get-tuple-element.41), channel_id=1, source_target_pairs={{0,16},{16,0},{32,48},{48,32},{64,80},{80,64},{96,112},{112,96},{1... | collective-permute-start | bytes 1544 | tf_op jit(solution)/shard_map/ppermute | solution.py:329

commit v3 on v2

--- a/solution.py
+++ b/solution.py
@@ -275,7 +275,7 @@
             lane = pl.multiple_of(device * ROWS + core * HALF, HALF)
             prims.append(ids_ref[0:1, pl.ds(lane, HALF)] - own * LISTS)
         prim = jnp.concatenate(prims, axis=1)
-        each = SIDE // n_arrays
+        each = len(steps) // n_arrays
         ref, at = arrays[n // each], n % each * 2 * ROWS
         parts = [ref[at + k * HALF : at + (k + 1) * HALF] for k in range(4)]
         head = jnp.concatenate([parts[0], parts[2]], axis=0)
@@ -301,11 +301,12 @@
         functools.partial(score_kernel, steps, len(arrays), len(last)),
         name,
         28,
-        out if len(last) == 2 else (out, jax.ShapeDtypeStruct((LISTS, 128), f32)),
+        (out, jax.ShapeDtypeStruct((LISTS, 128), f32)) if len(last) == 1 else out,
         ids,
         prefixes,
         *arrays,
         *last,
+        scratch=[] if last else [pltpu.VMEM((LISTS, 128), f32)],
     )
 
 
@@ -353,11 +354,11 @@
         move(pairs[k], STEPS[n], True) for k, n in ((0, 0), (1, 1), (1, 0), (0, 1))
     )
     steps = [[(a, d) for a in (0,) + STEPS] for d in (0,) + STEPS]
-    lowest, _ = scores("scores_near", ids, prefixes, blocks, steps[0])
+    lowest = scores("scores_near", ids, prefixes, blocks, steps[0])
     _, to_far, from_far, rows_in = together(lowest, ahead, behind, rows_in)
     far = [move(to_far, STEPS[0], True), move(from_far, STEPS[1], True)]
-    lowest, square = scores("scores_right", ids, prefixes, [ahead, ahead_too], steps[1], lowest)
-    lowest = scores("scores_left", ids, prefixes, [behind_too, behind], steps[2], lowest, square)
+    sides = [ahead, ahead_too, behind_too, behind]
+    lowest, square = scores("scores_sides", ids, prefixes, sides, steps[1] + steps[2], lowest)
     lowest = scores("scores_far", ids, prefixes, far, steps[3], lowest, square)
     back = lax.all_to_all(lowest, "list", 0, 0, tiled=True)
     placed = placement(id_rows, rows_in, parts)

time: 97.9 us -> 96.6 us (0.987)
  Pallas kernels: 39.5 us -> 37.3 us
  starting transfers between devices: 30.8 us -> 32.3 us
    all_to_all x1, starting transfers between devices: 6.16 us -> 9.26 us  [local(): rows_in = lax.all_to_all(rows_out, ('dp', 'list'), 0, 0, tiled=True)]
    pallas_call x8 -> x7, Pallas kernels: 39.5 us -> 37.3 us  [call(): pl.pallas_call(kernel, out_shape=out_shape, in_specs=[HBM if n in hbm els...]
    ppermute x9, starting transfers between devices: 12 us -> 10.6 us  [move(): return lax.ppermute(x, ('dp', 'list'), pairs)]
    ppermute x9, waiting for transfers between devices: 6.57 us -> 5.37 us  [move(): return lax.ppermute(x, ('dp', 'list'), pairs)]
  transfers between devices with their start and end apart: 14 -> 14, of which waited for: 7 -> 8; matrix products, arithmetic and copies ran while one was open for 3% -> 3% of each run, Pallas kernels for 31% -> 29%
where the time goes in v3:
time: 96.6 us; the launch traced here: 95 us
  Pallas kernels  37.3 us (39%)
  starting transfers between devices  32.3 us (33%)
  waiting for transfers between devices  18.2 us (19%)
  local copies, waits for them, and re-layouts  5.72 us (6%)
    pallas_call x7, Pallas kernels, call(): pl.pallas_call(kernel, out_shape=out_shape, in_specs=[HBM if n in hbm els...  37.3 us
    ppermute x9, starting transfers between devices, move(): return lax.ppermute(x, ('dp', 'list'), pairs)  10.6 us
    all_to_all x1, starting transfers between devices, local(): rows_in = lax.all_to_all(rows_out, ('dp', 'list'), 0, 0, tiled=True)  9.26 us
    all_to_all x1, starting transfers between devices, local(): got = lax.all_to_all(slots, 'list', 0, 0, tiled=True)  8.13 us
    ppermute x9, waiting for transfers between devices, move(): return lax.ppermute(x, ('dp', 'list'), pairs)  5.37 us
    all_to_all x1, waiting for transfers between devices, local(): back = lax.all_to_all(lowest, 'list', 0, 0, tiled=True)  5.28 us
    all_to_all x1, waiting for transfers between devices, local(): got = lax.all_to_all(slots, 'list', 0, 0, tiled=True)  4.5 us
    all_to_all x1, starting transfers between devices, local(): back = lax.all_to_all(lowest, 'list', 0, 0, tiled=True)  4.2 us
  transfers between devices with their start and end apart: 14, of which 8 were waited for; matrix products, arithmetic and copies ran while one was open for 3% of the time, Pallas kernels for 29%

profile of v3, /device:TPU:0, one launch (start us, length us, event | category | flops | bytes accessed | tf_op | source)
XLA Modules:
  0.0 95.0 jit_solution(17780475945633964924)
XLA Ops:
  0.6 0.0 copy-start
  0.6 1.8 %slice.12.c_ref.refs_1_ = bf16[4096,256]{1,0:T(8,128)(2,1)S(1)} slice(bf16[4096,768]{1,0:T(8,128)(2,1)} %c_hbm.1), slice={[0:4096], [0:256]} | slice | bytes 4194304 | tf_op jit(solution)/shard_map/slice | solution.py:341
  2.4 0.0 copy-done
  2.4 3.5 %pack_prefixes.1 = bf16[16,64,256]{2,1,0:T(8,128)(2,1)} custom-call(s32[2,32768]{1,0:T(2,128)S(1)} %bitcast.14, bf16[4096,256]{1,0:T(8,128)(2,1)S(1)} %slice.12.c_ref.refs_1_), custom_call_target="tpu_custom_call" | custom-call | tf_op jit(solution)/shard_map/pack_prefixes/pallas_call | solution.py:72
  6.0 8.1 %all-to-all-start = ((bf16[16,64,256]{2,1,0:T(8,128)(2,1)}), bf16[16,64,256]{2,1,0:T(8,128)(2,1)S(1)}, u32[]{:S(2)}, u32[]{:S(2)}) async-start(bf16[16,64,256]{2,1,0:T(8,128)(2,1)} %pack_prefixes.1), calls=%async_computation | async-start | bytes 1048576 | tf_op jit(solution)/shard_map/all_to_all | solution.py:343
  14.1 0.0 copy-start.1
  14.1 0.0 copy-start.2
  14.1 7.0 %prepare_rows.1 = (bf16[128,8,128]{2,1,0:T(8,128)(2,1)}, bf16[3,512,128]{2,1,0:T(8,128)(2,1)}) custom-call(s32[2,32768]{1,0:T(2,128)} %bitcast.13, bf16[4096,768]{1,0:T(8,128)(2,1)} %c_hbm.1, bf16[256,768]{1,0:T(8,128)(2,1)} %vec_hbm.3, bf16[768,128]{1,0:T(8,128)(2,1)} %proj_ref), custom_call_target="tpu_custom_call" | custom-call | tf_op jit(solution)/shard_map/prepare_rows/pallas_call | solution.py:72
  21.1 4.5 %all-to-all-done.got_ref = bf16[16,64,256]{2,1,0:T(8,128)(2,1)S(1)} async-done(((bf16[16,64,256]{2,1,0:T(8,128)(2,1)}), bf16[16,64,256]{2,1,0:T(8,128)(2,1)S(1)}, u32[]{:S(2)}, u32[]{:S(2)}) %all-to-all-start) | async-done | bytes 524320 | tf_op jit(solution)/shard_map/all_to_all | solution.py:343
  25.6 0.0 copy-done.1
  25.6 0.0 copy-done.2
  25.6 0.8 own_residuals.1
  26.4 0.1 collective-permute-start
  26.5 1.3 %collective-permute-done = bf16[256,256]{1,0:T(8,128)(2,1)S(1)} collective-permute-done((bf16[256,256]{1,0:T(8,128)(2,1)S(1)}, bf16[256,256]{1,0:T(8,128)(2,1)S(1)}, u32[]{:S(2)}, u32[]{:S(2)}) %collective-permute-start) | collective-permute-done | bytes 131104 | tf_op jit(solution)/shard_map/ppermute | solution.py:330
  27.8 0.7 collective-permute-start.2
  28.5 2.0 %collective-permute-start.3 = (bf16[512,256]{1,0:T(8,128)(2,1)S(1)}, bf16[512,256]{1,0:T(8,128)(2,1)S(1)}, u32[]{:S(2)}, u32[]{:S(2)}) collective-permute-start(bf16[512,256]{1,0:T(8,128)(2,1)S(1)} %pad_maximum_fusion.refs_2_), channel_id=1, source_target_pairs={{0,2},{1,3},{2,0},{3,1},{4,6},{5,7},{6,4},{7,5},{8,10},{9,11},{10,... | collective-permute-start | bytes 786440 | tf_op jit(solution)/shard_map/ppermute | solution.py:326
  30.5 0.0 collective-permute-start.1
  30.5 0.7 constant_dynamic-update-slice_fusion.1
  31.2 3.0 %collective-permute-done.2.refs_4_ = bf16[512,256]{1,0:T(8,128)(2,1)S(1)} collective-permute-done((bf16[512,256]{1,0:T(8,128)(2,1)S(1)}, bf16[512,256]{1,0:T(8,128)(2,1)S(1)}, u32[]{:S(2)}, u32[]{:S(2)}) %collective-permute-start.2) | collective-permute-done | bytes 262176 | tf_op jit(solution)/shard_map/ppermute | solution.py:326
  34.3 0.7 constant_dynamic-update-slice_fusion.3
  35.0 1.5 %collective-permute-done.3.refs_5_ = bf16[512,256]{1,0:T(8,128)(2,1)S(1)} collective-permute-done((bf16[512,256]{1,0:T(8,128)(2,1)S(1)}, bf16[512,256]{1,0:T(8,128)(2,1)S(1)}, u32[]{:S(2)}, u32[]{:S(2)}) %collective-permute-start.3) | collective-permute-done | bytes 262176 | tf_op jit(solution)/shard_map/ppermute | solution.py:326
  36.5 0.7 constant_dynamic-update-slice_fusion.2
  37.2 1.1 %collective-permute-start.5 = (bf16[1024,256]{1,0:T(8,128)(2,1)}, bf16[1024,256]{1,0:T(8,128)(2,1)}, u32[]{:S(2)}, u32[]{:S(2)}) collective-permute-start(bf16[1024,256]{1,0:T(8,128)(2,1)} %constant_dynamic-update-slice_fusion.2), channel_id=1, source_target_pairs={{0,12},{1,13},{2,14},{3,15},{4,0},{5,1},{6,2},{7,3},{8,4},{9,5},{1... | collective-permute-start | bytes 1572872 | tf_op jit(solution)/shard_map/ppermute | solution.py:326
  38.3 0.8 collective-permute-done.1.refs_3_
  39.2 0.8 constant_dynamic-update-slice_fusion
  40.0 0.2 collective-permute-start.4
  40.2 9.3 %all-to-all-start.1 = ((bf16[128,8,128]{2,1,0:T(8,128)(2,1)}), bf16[128,8,128]{2,1,0:T(8,128)(2,1)S(1)}, u32[]{:S(2)}, u32[]{:S(2)}) async-start(bf16[128,8,128]{2,1,0:T(8,128)(2,1)} %get-tuple-element.28), calls=%async_computation.1 | async-start | bytes 524288 | tf_op jit(solution)/shard_map/all_to_all | solution.py:351
  49.4 1.0 %collective-permute-start.8 = (bf16[1024,256]{1,0:T(8,128)(2,1)}, bf16[1024,256]{1,0:T(8,128)(2,1)}, u32[]{:S(2)}, u32[]{:S(2)}) collective-permute-start(bf16[1024,256]{1,0:T(8,128)(2,1)} %constant_dynamic-update-slice_fusion.2), channel_id=1, source_target_pairs={{0,4},{1,5},{2,6},{3,7},{4,8},{5,9},{6,10},{7,11},{8,12},{9,13},{1... | collective-permute-start | bytes 1572872 | tf_op jit(solution)/shard_map/ppermute | solution.py:326
  50.5 2.3 %collective-permute-start.9 = (bf16[1024,256]{1,0:T(8,128)(2,1)}, bf16[1024,256]{1,0:T(8,128)(2,1)}, u32[]{:S(2)}, u32[]{:S(2)}) collective-permute-start(bf16[1024,256]{1,0:T(8,128)(2,1)} %constant_dynamic-update-slice_fusion), channel_id=1, source_target_pairs={{0,12},{1,13},{2,14},{3,15},{4,0},{5,1},{6,2},{7,3},{8,4},{9,5},{1... | collective-permute-start | bytes 1572872 | tf_op jit(solution)/shard_map/ppermute | solution.py:326
  52.7 0.9 copy-done.4
  53.7 6.0 %scores_near.1.refs_6_ = f32[16,8,128]{2,1,0:T(8,128)S(1)} custom-call(s32[2,32768]{1,0:T(2,128)S(1)} %bitcast.16, bf16[4096,256]{1,0:T(8,128)(2,1)S(1)} %slice.12.c_ref.refs_1_, bf16[512,256]{1,0:T(8,128)(2,1)S(1)} %pad_maximum_fusion.refs_2_, bf16[512,256]{1,0:T(8,128)(2,1)S(1)} %copy-done.4, bf16[512,256]{1,0:T(8,128)(2,1)S(1)} %collective-permute-done.2.refs_4_, ...), custom_call_target="tpu_custom_call" | custom-call | tf_op jit(solution)/shard_map/scores_near/pallas_call | solution.py:72
  59.7 0.6 all-to-all-done.1.got_ref
  60.3 0.0 collective-permute-done.5.refs_5_
  60.3 0.0 collective-permute-done.4.refs_2_
  60.3 0.7 collective-permute-start.6
  61.1 2.5 %collective-permute-start.7 = (bf16[1024,256]{1,0:T(8,128)(2,1)}, bf16[1024,256]{1,0:T(8,128)(2,1)S(1)}, u32[]{:S(2)}, u32[]{:S(2)}) collective-permute-start(bf16[1024,256]{1,0:T(8,128)(2,1)} %collective-permute-done.5.refs_5_), channel_id=1, source_target_pairs={{0,12},{1,13},{2,14},{3,15},{4,0},{5,1},{6,2},{7,3},{8,4},{9,5},{1... | collective-permute-start | bytes 1572872 | tf_op jit(solution)/shard_map/ppermute | solution.py:326
  63.6 0.0 collective-permute-done.8.refs_3_
  63.6 0.0 collective-permute-done.9.refs_4_
  63.6 12.0 %scores_sides.1 = (f32[16,8,128]{2,1,0:T(8,128)S(1)}, f32[4096,128]{1,0:T(8,128)S(1)}) custom-call(s32[2,32768]{1,0:T(2,128)S(1)} %bitcast.17, bf16[4096,256]{1,0:T(8,128)(2,1)S(1)} %slice.12.c_ref.refs_1_, bf16[1024,256]{1,0:T(8,128)(2,1)} %collective-permute-done.4.refs_2_, bf16[1024,256]{1,0:T(8,128)(2,1)} %collective-permute-done.8.refs_3_, ...), custom_call_target="tpu_custom_call" | custom-call | tf_op jit(solution)/shard_map/scores_sides/pallas_call | solution.py:72
  75.5 0.0 collective-permute-done.6.refs_2_
  75.6 0.0 collective-permute-done.7.refs_3_
  75.6 5.7 %scores_far.1 = f32[16,8,128]{2,1,0:T(8,128)} custom-call(s32[2,32768]{1,0:T(2,128)S(1)} %bitcast.18, bf16[4096,256]{1,0:T(8,128)(2,1)S(1)} %slice.12.c_ref.refs_1_, bf16[1024,256]{1,0:T(8,128)(2,1)S(1)} %collective-permute-done.6.refs_2_, bf16[1024,256]{1,0:T(8,128)(2,1)S(1)} %collective-permute-done.7.refs_3_, ...), custom_call_target="tpu_custom_call" | custom-call | tf_op jit(solution)/shard_map/scores_far/pallas_call | solution.py:72
  81.3 4.2 %all-to-all-start.2 = ((f32[16,8,128]{2,1,0:T(8,128)}), f32[16,8,128]{2,1,0:T(8,128)S(1)}, u32[]{:S(2)}, u32[]{:S(2)}) async-start(f32[16,8,128]{2,1,0:T(8,128)} %scores_far.1), calls=%async_computation.2 | async-start | bytes 131072 | tf_op jit(solution)/shard_map/all_to_all | solution.py:363
  85.5 2.3 %place_rows.1 = bf16[1024,128]{1,0:T(8,128)(2,1)} custom-call(s32[2,128,256]{2,1,0:T(8,128)S(1)} %bitcast.20, bf16[128,8,128]{2,1,0:T(8,128)(2,1)S(1)} %all-to-all-done.1.got_ref, bf16[3,512,128]{2,1,0:T(8,128)(2,1)S(1)} %copy-done.5), custom_call_target="tpu_custom_call" | custom-call | tf_op jit(solution)/shard_map/place_rows/pallas_call | solution.py:72
  87.9 5.3 %all-to-all-done.2 = f32[16,8,128]{2,1,0:T(8,128)S(1)} async-done(((f32[16,8,128]{2,1,0:T(8,128)}), f32[16,8,128]{2,1,0:T(8,128)S(1)}, u32[]{:S(2)}, u32[]{:S(2)}) %all-to-all-start.2) | async-done | bytes 65568 | tf_op jit(solution)/shard_map/all_to_all | solution.py:363
  93.2 0.1 collective-permute-start.10
  93.3 1.1 %collective-permute-done.10 = f32[1,128]{1,0:T(1,128)S(1)} collective-permute-done((f32[1,128]{1,0:T(1,128)S(1)}, f32[1,128]{1,0:T(1,128)S(1)}, u32[]{:S(2)}, u32[]{:S(2)}) %collective-permute-start.10) | collective-permute-done | bytes 544 | tf_op jit(solution)/shard_map/ppermute | solution.py:330
  94.4 0.6 fusion
  (10 shorter events, 0.1 us)
Async XLA Ops:
  0.6 1.8 %copy-start = (s32[32768,2]{0,1:T(2,128)S(1)}, s32[32768,2]{0,1:T(2,128)}, u32[]{:S(2)}) copy-start(s32[32768,2]{0,1:T(2,128)} %param.7) | copy-start | bytes 786436
  6.0 19.6 %all-to-all-start = ((bf16[16,64,256]{2,1,0:T(8,128)(2,1)}), bf16[16,64,256]{2,1,0:T(8,128)(2,1)S(1)}, u32[]{:S(2)}, u32[]{:S(2)}) async-start(bf16[16,64,256]{2,1,0:T(8,128)(2,1)} %pack_prefixes.1), calls=%async_computation | async-start | bytes 1048576 | tf_op jit(solution)/shard_map/all_to_all | solution.py:343
  14.1 11.5 %copy-start.1 = (s32[32768,2]{0,1:T(2,128)S(1)}, s32[32768,2]{0,1:T(2,128)}, u32[]{:S(2)}) copy-start(s32[32768,2]{0,1:T(2,128)} %param.7) | copy-start | bytes 786436
  14.1 11.5 %copy-start.2 = (bf16[256,768]{1,0:T(8,128)(2,1)S(1)}, bf16[256,768]{1,0:T(8,128)(2,1)}, u32[]{:S(2)}) copy-start(bf16[256,768]{1,0:T(8,128)(2,1)} %vec_hbm.3) | copy-start | bytes 1179652
  26.4 1.4 %collective-permute-start = (bf16[256,256]{1,0:T(8,128)(2,1)S(1)}, bf16[256,256]{1,0:T(8,128)(2,1)S(1)}, u32[]{:S(2)}, u32[]{:S(2)}) collective-permute-start(bf16[256,256]{1,0:T(8,128)(2,1)S(1)} %get-tuple-element.25), channel_id=1, source_target_pairs={{0,16},{16,0},{32,48},{48,32},{64,80},{80,64},{96,112},{112,96},{1... | collective-permute-start | bytes 393224 | tf_op jit(solution)/shard_map/ppermute | solution.py:330
  27.8 6.4 %collective-permute-start.2 = (bf16[512,256]{1,0:T(8,128)(2,1)S(1)}, bf16[512,256]{1,0:T(8,128)(2,1)S(1)}, u32[]{:S(2)}, u32[]{:S(2)}) collective-permute-start(bf16[512,256]{1,0:T(8,128)(2,1)S(1)} %pad_maximum_fusion.refs_2_), channel_id=1, source_target_pairs={{0,3},{1,0},{2,1},{3,2},{4,7},{5,4},{6,5},{7,6},{8,11},{9,8},{10,9... | collective-permute-start | bytes 786440 | tf_op jit(solution)/shard_map/ppermute | solution.py:326
  28.5 8.0 %collective-permute-start.3 = (bf16[512,256]{1,0:T(8,128)(2,1)S(1)}, bf16[512,256]{1,0:T(8,128)(2,1)S(1)}, u32[]{:S(2)}, u32[]{:S(2)}) collective-permute-start(bf16[512,256]{1,0:T(8,128)(2,1)S(1)} %pad_maximum_fusion.refs_2_), channel_id=1, source_target_pairs={{0,2},{1,3},{2,0},{3,1},{4,6},{5,7},{6,4},{7,5},{8,10},{9,11},{10,... | collective-permute-start | bytes 786440 | tf_op jit(solution)/shard_map/ppermute | solution.py:326
  30.5 8.7 %collective-permute-start.1 = (bf16[512,256]{1,0:T(8,128)(2,1)S(1)}, bf16[512,256]{1,0:T(8,128)(2,1)S(1)}, u32[]{:S(2)}, u32[]{:S(2)}) collective-permute-start(bf16[512,256]{1,0:T(8,128)(2,1)S(1)} %pad_maximum_fusion.refs_2_), channel_id=1, source_target_pairs={{0,1},{1,2},{2,3},{3,0},{4,5},{5,6},{6,7},{7,4},{8,9},{9,10},{10,1... | collective-permute-start | bytes 786440 | tf_op jit(solution)/shard_map/ppermute | solution.py:326
  37.2 23.1 %collective-permute-start.5 = (bf16[1024,256]{1,0:T(8,128)(2,1)}, bf16[1024,256]{1,0:T(8,128)(2,1)}, u32[]{:S(2)}, u32[]{:S(2)}) collective-permute-start(bf16[1024,256]{1,0:T(8,128)(2,1)} %constant_dynamic-update-slice_fusion.2), channel_id=1, source_target_pairs={{0,12},{1,13},{2,14},{3,15},{4,0},{5,1},{6,2},{7,3},{8,4},{9,5},{1... | collective-permute-start | bytes 1572872 | tf_op jit(solution)/shard_map/ppermute | solution.py:326
  39.2 1.0 %copy-start.3 = (bf16[512,256]{1,0:T(8,128)(2,1)}, bf16[512,256]{1,0:T(8,128)(2,1)S(1)}, u32[]{:S(2)}) copy-start(bf16[512,256]{1,0:T(8,128)(2,1)S(1)} %collective-permute-done.1.refs_3_) | copy-start | bytes 786436
  40.0 20.4 %collective-permute-start.4 = (bf16[1024,256]{1,0:T(8,128)(2,1)}, bf16[1024,256]{1,0:T(8,128)(2,1)}, u32[]{:S(2)}, u32[]{:S(2)}) collective-permute-start(bf16[1024,256]{1,0:T(8,128)(2,1)} %constant_dynamic-update-slice_fusion), channel_id=1, source_target_pairs={{0,4},{1,5},{2,6},{3,7},{4,8},{5,9},{6,10},{7,11},{8,12},{9,13},{1... | collective-permute-start | bytes 1572872 | tf_op jit(solution)/shard_map/ppermute | solution.py:326
  40.2 20.2 %all-to-all-start.1 = ((bf16[128,8,128]{2,1,0:T(8,128)(2,1)}), bf16[128,8,128]{2,1,0:T(8,128)(2,1)S(1)}, u32[]{:S(2)}, u32[]{:S(2)}) async-start(bf16[128,8,128]{2,1,0:T(8,128)(2,1)} %get-tuple-element.28), calls=%async_computation.1 | async-start | bytes 524288 | tf_op jit(solution)/shard_map/all_to_all | solution.py:351
  49.4 14.1 %collective-permute-start.8 = (bf16[1024,256]{1,0:T(8,128)(2,1)}, bf16[1024,256]{1,0:T(8,128)(2,1)}, u32[]{:S(2)}, u32[]{:S(2)}) collective-permute-start(bf16[1024,256]{1,0:T(8,128)(2,1)} %constant_dynamic-update-slice_fusion.2), channel_id=1, source_target_pairs={{0,4},{1,5},{2,6},{3,7},{4,8},{5,9},{6,10},{7,11},{8,12},{9,13},{1... | collective-permute-start | bytes 1572872 | tf_op jit(solution)/shard_map/ppermute | solution.py:326
  50.5 13.1 %collective-permute-start.9 = (bf16[1024,256]{1,0:T(8,128)(2,1)}, bf16[1024,256]{1,0:T(8,128)(2,1)}, u32[]{:S(2)}, u32[]{:S(2)}) collective-permute-start(bf16[1024,256]{1,0:T(8,128)(2,1)} %constant_dynamic-update-slice_fusion), channel_id=1, source_target_pairs={{0,12},{1,13},{2,14},{3,15},{4,0},{5,1},{6,2},{7,3},{8,4},{9,5},{1... | collective-permute-start | bytes 1572872 | tf_op jit(solution)/shard_map/ppermute | solution.py:326
  52.7 0.9 copy-start.4
  60.3 15.2 %collective-permute-start.6 = (bf16[1024,256]{1,0:T(8,128)(2,1)}, bf16[1024,256]{1,0:T(8,128)(2,1)S(1)}, u32[]{:S(2)}, u32[]{:S(2)}) collective-permute-start(bf16[1024,256]{1,0:T(8,128)(2,1)} %collective-permute-done.4.refs_2_), channel_id=1, source_target_pairs={{0,4},{1,5},{2,6},{3,7},{4,8},{5,9},{6,10},{7,11},{8,12},{9,13},{1... | collective-permute-start | bytes 1572872 | tf_op jit(solution)/shard_map/ppermute | solution.py:326
  61.1 14.5 %collective-permute-start.7 = (bf16[1024,256]{1,0:T(8,128)(2,1)}, bf16[1024,256]{1,0:T(8,128)(2,1)S(1)}, u32[]{:S(2)}, u32[]{:S(2)}) collective-permute-start(bf16[1024,256]{1,0:T(8,128)(2,1)} %collective-permute-done.5.refs_5_), channel_id=1, source_target_pairs={{0,12},{1,13},{2,14},{3,15},{4,0},{5,1},{6,2},{7,3},{8,4},{9,5},{1... | collective-permute-start | bytes 1572872 | tf_op jit(solution)/shard_map/ppermute | solution.py:326
  75.6 10.0 %copy-start.5 = (bf16[3,512,128]{2,1,0:T(8,128)(2,1)S(1)}, bf16[3,512,128]{2,1,0:T(8,128)(2,1)}, u32[]{:S(2)}) copy-start(bf16[3,512,128]{2,1,0:T(8,128)(2,1)} %get-tuple-element.34.parts_ref) | copy-start | bytes 1179652
  81.3 11.9 %all-to-all-start.2 = ((f32[16,8,128]{2,1,0:T(8,128)}), f32[16,8,128]{2,1,0:T(8,128)S(1)}, u32[]{:S(2)}, u32[]{:S(2)}) async-start(f32[16,8,128]{2,1,0:T(8,128)} %scores_far.1), calls=%async_computation.2 | async-start | bytes 131072 | tf_op jit(solution)/shard_map/all_to_all | solution.py:363
  93.2 1.2 %collective-permute-start.10 = (f32[1,128]{1,0:T(1,128)S(1)}, f32[1,128]{1,0:T(1,128)S(1)}, u32[]{:S(2)}, u32[]{:S(2)}) collective-permute-start(f32[1,128]{1,0:T(1,128)S(1)} %get-tuple-element.39), channel_id=1, source_target_pairs={{0,16},{16,0},{32,48},{48,32},{64,80},{80,64},{96,112},{112,96},{1... | collective-permute-start | bytes 1544 | tf_op jit(solution)/shard_map/ppermute | solution.py:330

commit v4 on v3

--- a/solution.py
+++ b/solution.py
@@ -296,7 +296,7 @@
 
 
 def scores(name, ids, prefixes, arrays, steps, *last):
-    out = jax.ShapeDtypeStruct((N_LIST, 8, HALF), f32)
+    out = jax.ShapeDtypeStruct((N_LIST, 2, HALF), f32)
     return call(
         functools.partial(score_kernel, steps, len(arrays), len(last)),
         name,
@@ -350,12 +350,12 @@
     blocks = [block] + [move(block, d, False) for d in STEPS]
     rows_in = lax.all_to_all(rows_out, ("dp", "list"), 0, 0, tiled=True)
     pairs = [jnp.concatenate(blocks[k : k + 2], axis=0) for k in (0, 2)]
-    ahead, behind, ahead_too, behind_too = (
-        move(pairs[k], STEPS[n], True) for k, n in ((0, 0), (1, 1), (1, 0), (0, 1))
+    ahead, behind_too, behind, ahead_too = (
+        move(pairs[k], STEPS[n], True) for k, n in ((0, 0), (0, 1), (1, 1), (1, 0))
     )
     steps = [[(a, d) for a in (0,) + STEPS] for d in (0,) + STEPS]
     lowest = scores("scores_near", ids, prefixes, blocks, steps[0])
-    _, to_far, from_far, rows_in = together(lowest, ahead, behind, rows_in)
+    _, to_far, from_far, behind_too, rows_in = together(lowest, ahead, behind, behind_too, rows_in)
     far = [move(to_far, STEPS[0], True), move(from_far, STEPS[1], True)]
     sides = [ahead, ahead_too, behind_too, behind]
     lowest, square = scores("scores_sides", ids, prefixes, sides, steps[1] + steps[2], lowest)
@@ -363,7 +363,7 @@
     back = lax.all_to_all(lowest, "list", 0, 0, tiled=True)
     placed = placement(id_rows, rows_in, parts)
     back, placed = together(back, placed)
-    low = jnp.min(back[:, :2], axis=0)
+    low = jnp.min(back, axis=0)
     other = from_other_core(low[1:])
     core = lax.axis_index("dp") % 2
     low = jnp.where(iota((2, HALF), 0) == core, low[:1], other)

time: 96.6 us -> 96.3 us (level)
  starting transfers between devices: 32.3 us -> 30.1 us
  waiting for transfers between devices: 18.2 us -> 20.2 us
    all_to_all x1, starting transfers between devices: 9.26 us -> 6.79 us  [local(): rows_in = lax.all_to_all(rows_out, ('dp', 'list'), 0, 0, tiled=True)]
    all_to_all x1, waiting for transfers between devices: 0.62 us -> 2.71 us  [local(): rows_in = lax.all_to_all(rows_out, ('dp', 'list'), 0, 0, tiled=True)]
    ppermute x9, starting transfers between devices: 10.6 us -> 11.6 us  [move(): return lax.ppermute(x, ('dp', 'list'), pairs)]
where the time goes in v4:
time: 96.3 us; the launch traced here: 94.7 us
  Pallas kernels  37.2 us (39%)
  starting transfers between devices  30.1 us (31%)
  waiting for transfers between devices  20.2 us (21%)
  local copies, waits for them, and re-layouts  5.72 us (6%)
    pallas_call x7, Pallas kernels, call(): pl.pallas_call(kernel, out_shape=out_shape, in_specs=[HBM if n in hbm els...  37.2 us
    ppermute x9, starting transfers between devices, move(): return lax.ppermute(x, ('dp', 'list'), pairs)  11.6 us
    all_to_all x1, starting transfers between devices, local(): got = lax.all_to_all(slots, 'list', 0, 0, tiled=True)  8.13 us
    all_to_all x1, starting transfers between devices, local(): rows_in = lax.all_to_all(rows_out, ('dp', 'list'), 0, 0, tiled=True)  6.79 us
    ppermute x9, waiting for transfers between devices, move(): return lax.ppermute(x, ('dp', 'list'), pairs)  5.37 us
    all_to_all x1, waiting for transfers between devices, local(): back = lax.all_to_all(lowest, 'list', 0, 0, tiled=True)  5.15 us
    all_to_all x1, waiting for transfers between devices, local(): got = lax.all_to_all(slots, 'list', 0, 0, tiled=True)  4.5 us
    all_to_all x1, starting transfers between devices, local(): back = lax.all_to_all(lowest, 'list', 0, 0, tiled=True)  3.44 us
  transfers between devices with their start and end apart: 14, of which 8 were waited for; matrix products, arithmetic and copies ran while one was open for 3% of the time, Pallas kernels for 29%

profile of v4, /device:TPU:0, one launch (start us, length us, event | category | flops | bytes accessed | tf_op | source)
XLA Modules:
  0.0 94.7 jit_solution(10195798358049429842)
XLA Ops:
  0.6 0.0 copy-start
  0.6 1.8 %slice.9.c_ref.refs_1_ = bf16[4096,256]{1,0:T(8,128)(2,1)S(1)} slice(bf16[4096,768]{1,0:T(8,128)(2,1)} %c_hbm.1), slice={[0:4096], [0:256]} | slice | bytes 4194304 | tf_op jit(solution)/shard_map/slice | solution.py:341
  2.4 0.0 copy-done
  2.4 3.5 %pack_prefixes.1 = bf16[16,64,256]{2,1,0:T(8,128)(2,1)} custom-call(s32[2,32768]{1,0:T(2,128)S(1)} %bitcast.14, bf16[4096,256]{1,0:T(8,128)(2,1)S(1)} %slice.9.c_ref.refs_1_), custom_call_target="tpu_custom_call" | custom-call | tf_op jit(solution)/shard_map/pack_prefixes/pallas_call | solution.py:72
  6.0 8.1 %all-to-all-start = ((bf16[16,64,256]{2,1,0:T(8,128)(2,1)}), bf16[16,64,256]{2,1,0:T(8,128)(2,1)S(1)}, u32[]{:S(2)}, u32[]{:S(2)}) async-start(bf16[16,64,256]{2,1,0:T(8,128)(2,1)} %pack_prefixes.1), calls=%async_computation | async-start | bytes 1048576 | tf_op jit(solution)/shard_map/all_to_all | solution.py:343
  14.1 0.0 copy-start.1
  14.1 0.0 copy-start.2
  14.1 7.0 %prepare_rows.1 = (bf16[128,8,128]{2,1,0:T(8,128)(2,1)}, bf16[3,512,128]{2,1,0:T(8,128)(2,1)}) custom-call(s32[2,32768]{1,0:T(2,128)} %bitcast.13, bf16[4096,768]{1,0:T(8,128)(2,1)} %c_hbm.1, bf16[256,768]{1,0:T(8,128)(2,1)} %vec_hbm.3, bf16[768,128]{1,0:T(8,128)(2,1)} %proj_ref), custom_call_target="tpu_custom_call" | custom-call | tf_op jit(solution)/shard_map/prepare_rows/pallas_call | solution.py:72
  21.1 4.5 %all-to-all-done.got_ref = bf16[16,64,256]{2,1,0:T(8,128)(2,1)S(1)} async-done(((bf16[16,64,256]{2,1,0:T(8,128)(2,1)}), bf16[16,64,256]{2,1,0:T(8,128)(2,1)S(1)}, u32[]{:S(2)}, u32[]{:S(2)}) %all-to-all-start) | async-done | bytes 524320 | tf_op jit(solution)/shard_map/all_to_all | solution.py:343
  25.6 0.0 copy-done.1
  25.6 0.8 own_residuals.1
  26.4 0.1 collective-permute-start
  26.5 1.3 %collective-permute-done = bf16[256,256]{1,0:T(8,128)(2,1)S(1)} collective-permute-done((bf16[256,256]{1,0:T(8,128)(2,1)S(1)}, bf16[256,256]{1,0:T(8,128)(2,1)S(1)}, u32[]{:S(2)}, u32[]{:S(2)}) %collective-permute-start) | collective-permute-done | bytes 131104 | tf_op jit(solution)/shard_map/ppermute | solution.py:330
  27.8 0.7 collective-permute-start.2
  28.5 2.0 %collective-permute-start.3 = (bf16[512,256]{1,0:T(8,128)(2,1)S(1)}, bf16[512,256]{1,0:T(8,128)(2,1)S(1)}, u32[]{:S(2)}, u32[]{:S(2)}) collective-permute-start(bf16[512,256]{1,0:T(8,128)(2,1)S(1)} %pad_maximum_fusion.refs_2_), channel_id=1, source_target_pairs={{0,2},{1,3},{2,0},{3,1},{4,6},{5,7},{6,4},{7,5},{8,10},{9,11},{10,... | collective-permute-start | bytes 786440 | tf_op jit(solution)/shard_map/ppermute | solution.py:326
  30.5 0.0 collective-permute-start.1
  30.5 0.7 constant_dynamic-update-slice_fusion.1
  31.2 3.0 %collective-permute-done.2.refs_4_ = bf16[512,256]{1,0:T(8,128)(2,1)S(1)} collective-permute-done((bf16[512,256]{1,0:T(8,128)(2,1)S(1)}, bf16[512,256]{1,0:T(8,128)(2,1)S(1)}, u32[]{:S(2)}, u32[]{:S(2)}) %collective-permute-start.2) | collective-permute-done | bytes 262176 | tf_op jit(solution)/shard_map/ppermute | solution.py:326
  34.3 0.7 constant_dynamic-update-slice_fusion.3
  35.0 1.5 %collective-permute-done.3.refs_5_ = bf16[512,256]{1,0:T(8,128)(2,1)S(1)} collective-permute-done((bf16[512,256]{1,0:T(8,128)(2,1)S(1)}, bf16[512,256]{1,0:T(8,128)(2,1)S(1)}, u32[]{:S(2)}, u32[]{:S(2)}) %collective-permute-start.3) | collective-permute-done | bytes 262176 | tf_op jit(solution)/shard_map/ppermute | solution.py:326
  36.5 0.7 constant_dynamic-update-slice_fusion.2
  37.2 1.1 %collective-permute-start.5 = (bf16[1024,256]{1,0:T(8,128)(2,1)}, bf16[1024,256]{1,0:T(8,128)(2,1)}, u32[]{:S(2)}, u32[]{:S(2)}) collective-permute-start(bf16[1024,256]{1,0:T(8,128)(2,1)} %constant_dynamic-update-slice_fusion.2), channel_id=1, source_target_pairs={{0,12},{1,13},{2,14},{3,15},{4,0},{5,1},{6,2},{7,3},{8,4},{9,5},{1... | collective-permute-start | bytes 1572872 | tf_op jit(solution)/shard_map/ppermute | solution.py:326
  38.3 0.8 collective-permute-done.1.refs_3_
  39.2 0.8 constant_dynamic-update-slice_fusion
  40.0 0.2 collective-permute-start.4
  40.2 3.0 %collective-permute-start.6 = (bf16[1024,256]{1,0:T(8,128)(2,1)}, bf16[1024,256]{1,0:T(8,128)(2,1)}, u32[]{:S(2)}, u32[]{:S(2)}) collective-permute-start(bf16[1024,256]{1,0:T(8,128)(2,1)} %constant_dynamic-update-slice_fusion), channel_id=1, source_target_pairs={{0,12},{1,13},{2,14},{3,15},{4,0},{5,1},{6,2},{7,3},{8,4},{9,5},{1... | collective-permute-start | bytes 1572872 | tf_op jit(solution)/shard_map/ppermute | solution.py:326
  43.2 6.8 %all-to-all-start.1 = ((bf16[128,8,128]{2,1,0:T(8,128)(2,1)}), bf16[128,8,128]{2,1,0:T(8,128)(2,1)S(1)}, u32[]{:S(2)}, u32[]{:S(2)}) async-start(bf16[128,8,128]{2,1,0:T(8,128)(2,1)} %get-tuple-element.29), calls=%async_computation.1 | async-start | bytes 524288 | tf_op jit(solution)/shard_map/all_to_all | solution.py:351
  50.0 1.2 %collective-permute-start.9 = (bf16[1024,256]{1,0:T(8,128)(2,1)}, bf16[1024,256]{1,0:T(8,128)(2,1)}, u32[]{:S(2)}, u32[]{:S(2)}) collective-permute-start(bf16[1024,256]{1,0:T(8,128)(2,1)} %constant_dynamic-update-slice_fusion.2), channel_id=1, source_target_pairs={{0,4},{1,5},{2,6},{3,7},{4,8},{5,9},{6,10},{7,11},{8,12},{9,13},{1... | collective-permute-start | bytes 1572872 | tf_op jit(solution)/shard_map/ppermute | solution.py:326
  51.2 0.9 %copy-done.4 = bf16[512,256]{1,0:T(8,128)(2,1)S(1)} copy-done((bf16[512,256]{1,0:T(8,128)(2,1)S(1)}, bf16[512,256]{1,0:T(8,128)(2,1)}, u32[]{:S(2)}) %copy-start.4) | copy-done | bytes 262168
  52.2 6.0 %scores_near.1.refs_6_ = f32[16,2,128]{2,1,0:T(2,128)S(1)} custom-call(s32[2,32768]{1,0:T(2,128)S(1)} %bitcast.16, bf16[4096,256]{1,0:T(8,128)(2,1)S(1)} %slice.9.c_ref.refs_1_, bf16[512,256]{1,0:T(8,128)(2,1)S(1)} %pad_maximum_fusion.refs_2_, bf16[512,256]{1,0:T(8,128)(2,1)S(1)} %copy-done.4, bf16[512,256]{1,0:T(8,128)(2,1)S(1)} %collective-permute-done.2.refs_4_, ...), custom_call_target="tpu_custom_call" | custom-call | tf_op jit(solution)/shard_map/scores_near/pallas_call | solution.py:72
  58.2 2.7 %all-to-all-done.1.got_ref = bf16[128,8,128]{2,1,0:T(8,128)(2,1)S(1)} async-done(((bf16[128,8,128]{2,1,0:T(8,128)(2,1)}), bf16[128,8,128]{2,1,0:T(8,128)(2,1)S(1)}, u32[]{:S(2)}, u32[]{:S(2)}) %all-to-all-start.1) | async-done | bytes 262176 | tf_op jit(solution)/shard_map/all_to_all | solution.py:351
  60.9 0.0 collective-permute-done.5.refs_5_
  60.9 0.0 collective-permute-done.4.refs_2_
  60.9 0.0 collective-permute-done.6.refs_4_
  60.9 0.8 collective-permute-start.7
  61.7 2.5 %collective-permute-start.8 = (bf16[1024,256]{1,0:T(8,128)(2,1)}, bf16[1024,256]{1,0:T(8,128)(2,1)S(1)}, u32[]{:S(2)}, u32[]{:S(2)}) collective-permute-start(bf16[1024,256]{1,0:T(8,128)(2,1)} %collective-permute-done.5.refs_5_), channel_id=1, source_target_pairs={{0,12},{1,13},{2,14},{3,15},{4,0},{5,1},{6,2},{7,3},{8,4},{9,5},{1... | collective-permute-start | bytes 1572872 | tf_op jit(solution)/shard_map/ppermute | solution.py:326
  64.2 0.0 collective-permute-done.9.refs_3_
  64.2 12.0 %scores_sides.1 = (f32[16,2,128]{2,1,0:T(2,128)S(1)}, f32[4096,128]{1,0:T(8,128)S(1)}) custom-call(s32[2,32768]{1,0:T(2,128)S(1)} %bitcast.17, bf16[4096,256]{1,0:T(8,128)(2,1)S(1)} %slice.9.c_ref.refs_1_, bf16[1024,256]{1,0:T(8,128)(2,1)} %collective-permute-done.4.refs_2_, bf16[1024,256]{1,0:T(8,128)(2,1)} %collective-permute-done.9.refs_3_, ...), custom_call_target="tpu_custom_call" | custom-call | tf_op jit(solution)/shard_map/scores_sides/pallas_call | solution.py:72
  76.2 0.0 collective-permute-done.7.refs_2_
  76.2 0.0 collective-permute-done.8.refs_3_
  76.2 0.0 copy-start.5
  76.2 5.7 %scores_far.1 = f32[16,2,128]{2,1,0:T(2,128)} custom-call(s32[2,32768]{1,0:T(2,128)S(1)} %bitcast.18, bf16[4096,256]{1,0:T(8,128)(2,1)S(1)} %slice.9.c_ref.refs_1_, bf16[1024,256]{1,0:T(8,128)(2,1)S(1)} %collective-permute-done.7.refs_2_, bf16[1024,256]{1,0:T(8,128)(2,1)S(1)} %collective-permute-done.8.refs_3_, f32[16,2,128]{2,1,0:T(2,128)S(1)} %get-tuple-element.33.refs_4_, ...), custom_call_target="tpu_custom_call" | custom-call | tf_op jit(solution)/shard_map/scores_far/pallas_call | solution.py:72
  81.9 3.4 %all-to-all-start.2 = ((f32[16,2,128]{2,1,0:T(2,128)}), f32[16,2,128]{2,1,0:T(2,128)S(1)}, u32[]{:S(2)}, u32[]{:S(2)}) async-start(f32[16,2,128]{2,1,0:T(2,128)} %scores_far.1), calls=%async_computation.2 | async-start | bytes 32768 | tf_op jit(solution)/shard_map/all_to_all | solution.py:363
  85.4 2.3 %place_rows.1 = bf16[1024,128]{1,0:T(8,128)(2,1)} custom-call(s32[2,128,256]{2,1,0:T(8,128)S(1)} %bitcast.20, bf16[128,8,128]{2,1,0:T(8,128)(2,1)S(1)} %all-to-all-done.1.got_ref, bf16[3,512,128]{2,1,0:T(8,128)(2,1)S(1)} %copy-done.5), custom_call_target="tpu_custom_call" | custom-call | tf_op jit(solution)/shard_map/place_rows/pallas_call | solution.py:72
  87.7 5.2 %all-to-all-done.2 = f32[16,2,128]{2,1,0:T(2,128)S(1)} async-done(((f32[16,2,128]{2,1,0:T(2,128)}), f32[16,2,128]{2,1,0:T(2,128)S(1)}, u32[]{:S(2)}, u32[]{:S(2)}) %all-to-all-start.2) | async-done | bytes 16416 | tf_op jit(solution)/shard_map/all_to_all | solution.py:363
  92.9 0.1 collective-permute-start.10
  93.0 1.1 %collective-permute-done.10 = f32[1,128]{1,0:T(1,128)S(1)} collective-permute-done((f32[1,128]{1,0:T(1,128)S(1)}, f32[1,128]{1,0:T(1,128)S(1)}, u32[]{:S(2)}, u32[]{:S(2)}) %collective-permute-start.10) | collective-permute-done | bytes 544 | tf_op jit(solution)/shard_map/ppermute | solution.py:330
  94.1 0.6 fusion
  (10 shorter events, 0.1 us)
Async XLA Ops:
  0.6 1.8 %copy-start = (s32[32768,2]{0,1:T(2,128)S(1)}, s32[32768,2]{0,1:T(2,128)}, u32[]{:S(2)}) copy-start(s32[32768,2]{0,1:T(2,128)} %param.7) | copy-start | bytes 786436
  6.0 19.6 %all-to-all-start = ((bf16[16,64,256]{2,1,0:T(8,128)(2,1)}), bf16[16,64,256]{2,1,0:T(8,128)(2,1)S(1)}, u32[]{:S(2)}, u32[]{:S(2)}) async-start(bf16[16,64,256]{2,1,0:T(8,128)(2,1)} %pack_prefixes.1), calls=%async_computation | async-start | bytes 1048576 | tf_op jit(solution)/shard_map/all_to_all | solution.py:343
  14.1 11.5 %copy-start.1 = (s32[32768,2]{0,1:T(2,128)S(1)}, s32[32768,2]{0,1:T(2,128)}, u32[]{:S(2)}) copy-start(s32[32768,2]{0,1:T(2,128)} %param.7) | copy-start | bytes 786436
  14.1 11.5 %copy-start.2 = (bf16[256,768]{1,0:T(8,128)(2,1)S(1)}, bf16[256,768]{1,0:T(8,128)(2,1)}, u32[]{:S(2)}) copy-start(bf16[256,768]{1,0:T(8,128)(2,1)} %vec_hbm.3) | copy-start | bytes 1179652
  26.4 1.4 %collective-permute-start = (bf16[256,256]{1,0:T(8,128)(2,1)S(1)}, bf16[256,256]{1,0:T(8,128)(2,1)S(1)}, u32[]{:S(2)}, u32[]{:S(2)}) collective-permute-start(bf16[256,256]{1,0:T(8,128)(2,1)S(1)} %get-tuple-element.26), channel_id=1, source_target_pairs={{0,16},{16,0},{32,48},{48,32},{64,80},{80,64},{96,112},{112,96},{1... | collective-permute-start | bytes 393224 | tf_op jit(solution)/shard_map/ppermute | solution.py:330
  27.8 6.4 %collective-permute-start.2 = (bf16[512,256]{1,0:T(8,128)(2,1)S(1)}, bf16[512,256]{1,0:T(8,128)(2,1)S(1)}, u32[]{:S(2)}, u32[]{:S(2)}) collective-permute-start(bf16[512,256]{1,0:T(8,128)(2,1)S(1)} %pad_maximum_fusion.refs_2_), channel_id=1, source_target_pairs={{0,3},{1,0},{2,1},{3,2},{4,7},{5,4},{6,5},{7,6},{8,11},{9,8},{10,9... | collective-permute-start | bytes 786440 | tf_op jit(solution)/shard_map/ppermute | solution.py:326
  28.5 8.0 %collective-permute-start.3 = (bf16[512,256]{1,0:T(8,128)(2,1)S(1)}, bf16[512,256]{1,0:T(8,128)(2,1)S(1)}, u32[]{:S(2)}, u32[]{:S(2)}) collective-permute-start(bf16[512,256]{1,0:T(8,128)(2,1)S(1)} %pad_maximum_fusion.refs_2_), channel_id=1, source_target_pairs={{0,2},{1,3},{2,0},{3,1},{4,6},{5,7},{6,4},{7,5},{8,10},{9,11},{10,... | collective-permute-start | bytes 786440 | tf_op jit(solution)/shard_map/ppermute | solution.py:326
  30.5 8.7 %collective-permute-start.1 = (bf16[512,256]{1,0:T(8,128)(2,1)S(1)}, bf16[512,256]{1,0:T(8,128)(2,1)S(1)}, u32[]{:S(2)}, u32[]{:S(2)}) collective-permute-start(bf16[512,256]{1,0:T(8,128)(2,1)S(1)} %pad_maximum_fusion.refs_2_), channel_id=1, source_target_pairs={{0,1},{1,2},{2,3},{3,0},{4,5},{5,6},{6,7},{7,4},{8,9},{9,10},{10,1... | collective-permute-start | bytes 786440 | tf_op jit(solution)/shard_map/ppermute | solution.py:326
  37.2 23.7 %collective-permute-start.5 = (bf16[1024,256]{1,0:T(8,128)(2,1)}, bf16[1024,256]{1,0:T(8,128)(2,1)}, u32[]{:S(2)}, u32[]{:S(2)}) collective-permute-start(bf16[1024,256]{1,0:T(8,128)(2,1)} %constant_dynamic-update-slice_fusion.2), channel_id=1, source_target_pairs={{0,12},{1,13},{2,14},{3,15},{4,0},{5,1},{6,2},{7,3},{8,4},{9,5},{1... | collective-permute-start | bytes 1572872 | tf_op jit(solution)/shard_map/ppermute | solution.py:326
  39.2 4.0 %copy-start.3 = (bf16[512,256]{1,0:T(8,128)(2,1)}, bf16[512,256]{1,0:T(8,128)(2,1)S(1)}, u32[]{:S(2)}) copy-start(bf16[512,256]{1,0:T(8,128)(2,1)S(1)} %collective-permute-done.1.refs_3_) | copy-start | bytes 786436
  40.0 20.9 %collective-permute-start.4 = (bf16[1024,256]{1,0:T(8,128)(2,1)}, bf16[1024,256]{1,0:T(8,128)(2,1)}, u32[]{:S(2)}, u32[]{:S(2)}) collective-permute-start(bf16[1024,256]{1,0:T(8,128)(2,1)} %constant_dynamic-update-slice_fusion), channel_id=1, source_target_pairs={{0,4},{1,5},{2,6},{3,7},{4,8},{5,9},{6,10},{7,11},{8,12},{9,13},{1... | collective-permute-start | bytes 1572872 | tf_op jit(solution)/shard_map/ppermute | solution.py:326
  40.2 20.7 %collective-permute-start.6 = (bf16[1024,256]{1,0:T(8,128)(2,1)}, bf16[1024,256]{1,0:T(8,128)(2,1)}, u32[]{:S(2)}, u32[]{:S(2)}) collective-permute-start(bf16[1024,256]{1,0:T(8,128)(2,1)} %constant_dynamic-update-slice_fusion), channel_id=1, source_target_pairs={{0,12},{1,13},{2,14},{3,15},{4,0},{5,1},{6,2},{7,3},{8,4},{9,5},{1... | collective-permute-start | bytes 1572872 | tf_op jit(solution)/shard_map/ppermute | solution.py:326
  43.2 17.7 %all-to-all-start.1 = ((bf16[128,8,128]{2,1,0:T(8,128)(2,1)}), bf16[128,8,128]{2,1,0:T(8,128)(2,1)S(1)}, u32[]{:S(2)}, u32[]{:S(2)}) async-start(bf16[128,8,128]{2,1,0:T(8,128)(2,1)} %get-tuple-element.29), calls=%async_computation.1 | async-start | bytes 524288 | tf_op jit(solution)/shard_map/all_to_all | solution.py:351
  50.0 14.2 %collective-permute-start.9 = (bf16[1024,256]{1,0:T(8,128)(2,1)}, bf16[1024,256]{1,0:T(8,128)(2,1)}, u32[]{:S(2)}, u32[]{:S(2)}) collective-permute-start(bf16[1024,256]{1,0:T(8,128)(2,1)} %constant_dynamic-update-slice_fusion.2), channel_id=1, source_target_pairs={{0,4},{1,5},{2,6},{3,7},{4,8},{5,9},{6,10},{7,11},{8,12},{9,13},{1... | collective-permute-start | bytes 1572872 | tf_op jit(solution)/shard_map/ppermute | solution.py:326
  51.2 0.9 %copy-start.4 = (bf16[512,256]{1,0:T(8,128)(2,1)S(1)}, bf16[512,256]{1,0:T(8,128)(2,1)}, u32[]{:S(2)}) copy-start(bf16[512,256]{1,0:T(8,128)(2,1)} %copy-done.3) | copy-start | bytes 786436
  60.9 15.3 %collective-permute-start.7 = (bf16[1024,256]{1,0:T(8,128)(2,1)}, bf16[1024,256]{1,0:T(8,128)(2,1)S(1)}, u32[]{:S(2)}, u32[]{:S(2)}) collective-permute-start(bf16[1024,256]{1,0:T(8,128)(2,1)} %collective-permute-done.4.refs_2_), channel_id=1, source_target_pairs={{0,4},{1,5},{2,6},{3,7},{4,8},{5,9},{6,10},{7,11},{8,12},{9,13},{1... | collective-permute-start | bytes 1572872 | tf_op jit(solution)/shard_map/ppermute | solution.py:326
  61.7 14.5 %collective-permute-start.8 = (bf16[1024,256]{1,0:T(8,128)(2,1)}, bf16[1024,256]{1,0:T(8,128)(2,1)S(1)}, u32[]{:S(2)}, u32[]{:S(2)}) collective-permute-start(bf16[1024,256]{1,0:T(8,128)(2,1)} %collective-permute-done.5.refs_5_), channel_id=1, source_target_pairs={{0,12},{1,13},{2,14},{3,15},{4,0},{5,1},{6,2},{7,3},{8,4},{9,5},{1... | collective-permute-start | bytes 1572872 | tf_op jit(solution)/shard_map/ppermute | solution.py:326
  76.2 9.2 %copy-start.5 = (bf16[3,512,128]{2,1,0:T(8,128)(2,1)S(1)}, bf16[3,512,128]{2,1,0:T(8,128)(2,1)}, u32[]{:S(2)}) copy-start(bf16[3,512,128]{2,1,0:T(8,128)(2,1)} %get-tuple-element.36.parts_ref) | copy-start | bytes 1179652
  81.9 11.0 %all-to-all-start.2 = ((f32[16,2,128]{2,1,0:T(2,128)}), f32[16,2,128]{2,1,0:T(2,128)S(1)}, u32[]{:S(2)}, u32[]{:S(2)}) async-start(f32[16,2,128]{2,1,0:T(2,128)} %scores_far.1), calls=%async_computation.2 | async-start | bytes 32768 | tf_op jit(solution)/shard_map/all_to_all | solution.py:363
  92.9 1.2 %collective-permute-start.10 = (f32[1,128]{1,0:T(1,128)S(1)}, f32[1,128]{1,0:T(1,128)S(1)}, u32[]{:S(2)}, u32[]{:S(2)}) collective-permute-start(f32[1,128]{1,0:T(1,128)S(1)} %get-tuple-element.41), channel_id=1, source_target_pairs={{0,16},{16,0},{32,48},{48,32},{64,80},{80,64},{96,112},{112,96},{1... | collective-permute-start | bytes 1544 | tf_op jit(solution)/shard_map/ppermute | solution.py:330
